TPU v7x, 512 devices: a whole 4x4x16 slice. The times are simulated.
512 devices in a mesh: seq: 64 (over z, y), head: 8 (over x, core).
Axes of the slice: x: 4, y: 4, z: 16, core: 2. Of those that a mesh axis runs over, the one named last changes fastest.
Arguments:
- student_query: bfloat16 [8192, 64, 576], P('seq', 'head'), may hold values from -256 to 256
- teacher_query: bfloat16 [8192, 64, 576], P('seq', 'head'), may hold values from -256 to 256
- student_keys: bfloat16 [8192, 576], P('seq'), may hold values from -4 to 4
- teacher_keys: bfloat16 [8192, 576], P('seq'), may hold values from -4 to 4
- loss_weight: float32 [8192, 64], P('seq', 'head'), may hold values from 4 to 40
- doc_lengths: int32 [16], replicated, may hold values from 1 to 896, 8192 in all
Outputs:
- query_grad: bfloat16 [8192, 64, 576], P('seq', 'head')
- key_grad: bfloat16 [8192, 576], P('seq')
Inputs may be any that keep to these rules, and one draw needn't show every extreme that they name: `doc_lengths`: the lengths sum to 8192 and the longest is exactly 896.
All inputs are finite; a program needn't handle non-finite values.
Results may differ from a plain program's by a relative error of at most 0.012.
Values may be sent and summed in bfloat16 or wider, within the bound.
No kernel may reach another device: no remote copies, remote signals or barrier semaphores. Data moves between devices by JAX's collectives and lax.ppermute only.
A program may use at most 64 MiB of HBM per device.

v0:
```python
import jax
import jax.numpy as jnp
from jax import lax
from jax.sharding import PartitionSpec as P

SPAN = 7


score_scale = 192.0 ** (-0.5)


def from_behind(block, axis, distance):
    devices = range(lax.axis_size(axis))
    route = [(i - distance, i) for i in devices if i - distance in devices]
    return lax.ppermute(block, axis, route)


def doc_index(positions, doc_lengths):
    ends = jnp.cumsum(doc_lengths)
    return jnp.sum((positions[:, None] >= ends[None, :]).astype(jnp.int32), axis=1)


def masked_softmax(scores, visible):
    peak = jnp.max(jnp.where(visible, scores, -jnp.inf), axis=-1, keepdims=True)
    expo = jnp.where(visible, jnp.exp(scores - peak), 0.0)
    return expo / jnp.sum(expo, axis=-1, keepdims=True)


def on_device(student_query, teacher_query, student_keys, teacher_keys, loss_weight, doc_lengths):
    tok_rows = student_keys.shape[0]
    key_width = student_keys.shape[1]
    device = lax.axis_index("seq")
    pieces_s = [student_keys]
    pieces_t = [teacher_keys]
    for distance in range(1, SPAN + 1):
        got_s, got_t = from_behind((student_keys, teacher_keys), "seq", distance)
        pieces_s.append(got_s)
        pieces_t.append(got_t)
    window_s = jnp.stack(pieces_s, axis=0)
    window_t = jnp.stack(pieces_t, axis=0)
    keys_s = window_s.reshape(-1, key_width)
    keys_t = window_t.reshape(-1, key_width)
    owners = device - jnp.arange(SPAN + 1, dtype=jnp.int32)
    key_pos = (owners[:, None] * tok_rows + jnp.arange(tok_rows, dtype=jnp.int32)[None, :]).reshape(
        -1
    )
    query_pos = device * tok_rows + jnp.arange(tok_rows, dtype=jnp.int32)
    query_doc = doc_index(query_pos, doc_lengths)
    key_doc = doc_index(key_pos, doc_lengths)
    visible = (
        (query_doc[:, None] == key_doc[None, :])
        & (key_pos[None, :] <= query_pos[:, None])
        & (key_pos[None, :] >= 0)
    )
    visible = visible[:, None, :]
    student_scores = (
        jnp.einsum("thc,kc->thk", student_query, keys_s, preferred_element_type=jnp.float32)
        * score_scale
    )
    teacher_scores = (
        jnp.einsum("thc,kc->thk", teacher_query, keys_t, preferred_element_type=jnp.float32)
        * score_scale
    )
    student_probs = masked_softmax(student_scores, visible)
    teacher_probs = masked_softmax(teacher_scores, visible)
    score_grad = (loss_weight[:, :, None] * (student_probs - teacher_probs) * score_scale).astype(
        jnp.bfloat16
    )
    query_grad = jnp.einsum(
        "thk,kc->thc", score_grad, keys_s, preferred_element_type=jnp.float32
    ).astype(jnp.bfloat16)
    partial_value = jnp.einsum(
        "thk,thc->kc", score_grad, student_query, preferred_element_type=jnp.float32
    )
    partial_value = partial_value.reshape(SPAN + 1, tok_rows, key_width)
    summed = partial_value[0]
    for distance in range(1, SPAN + 1):
        summed = summed + from_behind(partial_value[distance], "seq", -distance)
    key_grad = lax.psum(summed, "head").astype(jnp.bfloat16)
    return (query_grad, key_grad)


def solution(mesh):
    return jax.shard_map(
        on_device,
        mesh=mesh,
        in_specs=(
            P("seq", "head", None),
            P("seq", "head", None),
            P("seq", None),
            P("seq", None),
            P("seq", "head"),
            P(),
        ),
        out_specs=(P("seq", "head", None), P("seq", None)),
        check_vma=False,
    )
```

profile of v0, /device:TPU:80, one launch (start us, length us, event | category | flops | bytes accessed | tf_op | source)
XLA Modules:
  0.0 237.9 jit_solution(10467859688748227027)
XLA Ops:
  0.7 4.7 %collective-permute-start.4 = (bf16[128,576]{0,1:T(8,128)(2,1)}, bf16[128,576]{0,1:T(8,128)(2,1)}, u32[]{:S(2)}, u32[]{:S(2)}) collective-permute-start(bf16[128,576]{0,1:T(8,128)(2,1)} %param.8), channel_id=1, source_target_pairs={{0,40},{8,48},{16,56},{24,64},{32,72},{40,80},{48,88},{56,96},{64,... | collective-permute-start | bytes 442376 | tf_op jit(solution)/shard_map/ppermute | solution.py:15
  5.3 5.0 %collective-permute-start.3 = (bf16[128,576]{0,1:T(8,128)(2,1)}, bf16[128,576]{0,1:T(8,128)(2,1)}, u32[]{:S(2)}, u32[]{:S(2)}) collective-permute-start(bf16[128,576]{0,1:T(8,128)(2,1)} %param.8), channel_id=1, source_target_pairs={{0,32},{8,40},{16,48},{24,56},{32,64},{40,72},{48,80},{56,88},{64,... | collective-permute-start | bytes 442376 | tf_op jit(solution)/shard_map/ppermute | solution.py:15
  10.4 4.0 %collective-permute-start.2 = (bf16[128,576]{0,1:T(8,128)(2,1)}, bf16[128,576]{0,1:T(8,128)(2,1)}, u32[]{:S(2)}, u32[]{:S(2)}) collective-permute-start(bf16[128,576]{0,1:T(8,128)(2,1)} %param.8), channel_id=1, source_target_pairs={{0,24},{8,32},{16,40},{24,48},{32,56},{40,64},{48,72},{56,80},{64,... | collective-permute-start | bytes 442376 | tf_op jit(solution)/shard_map/ppermute | solution.py:15
  14.4 4.8 %collective-permute-start.1 = (bf16[128,576]{0,1:T(8,128)(2,1)}, bf16[128,576]{0,1:T(8,128)(2,1)}, u32[]{:S(2)}, u32[]{:S(2)}) collective-permute-start(bf16[128,576]{0,1:T(8,128)(2,1)} %param.8), channel_id=1, source_target_pairs={{0,16},{8,24},{16,32},{24,40},{32,48},{40,56},{48,64},{56,72},{64,... | collective-permute-start | bytes 442376 | tf_op jit(solution)/shard_map/ppermute | solution.py:15
  19.2 2.9 %collective-permute-start.7 = (bf16[128,576]{0,1:T(8,128)(2,1)}, bf16[128,576]{0,1:T(8,128)(2,1)S(1)}, u32[]{:S(2)}, u32[]{:S(2)}) collective-permute-start(bf16[128,576]{0,1:T(8,128)(2,1)} %param.9), channel_id=1, source_target_pairs={{0,8},{8,16},{16,24},{24,32},{32,40},{40,48},{48,56},{56,64},{64,7... | collective-permute-start | bytes 442376 | tf_op jit(solution)/shard_map/ppermute | solution.py:15
  27.4 5.1 %collective-permute-start.8 = (bf16[128,576]{0,1:T(8,128)(2,1)}, bf16[128,576]{0,1:T(8,128)(2,1)S(1)}, u32[]{:S(2)}, u32[]{:S(2)}) collective-permute-start(bf16[128,576]{0,1:T(8,128)(2,1)} %param.9), channel_id=1, source_target_pairs={{0,16},{8,24},{16,32},{24,40},{32,48},{40,56},{48,64},{56,72},{64,... | collective-permute-start | bytes 442376 | tf_op jit(solution)/shard_map/ppermute | solution.py:15
  33.2 3.0 %collective-permute-done.8 = bf16[128,576]{0,1:T(8,128)(2,1)S(1)} collective-permute-done((bf16[128,576]{0,1:T(8,128)(2,1)}, bf16[128,576]{0,1:T(8,128)(2,1)S(1)}, u32[]{:S(2)}, u32[]{:S(2)}) %collective-permute-start.8) | collective-permute-done | bytes 147488 | tf_op jit(solution)/shard_map/ppermute | solution.py:15
  36.1 5.2 %collective-permute-start.9 = (bf16[128,576]{0,1:T(8,128)(2,1)}, bf16[128,576]{0,1:T(8,128)(2,1)S(1)}, u32[]{:S(2)}, u32[]{:S(2)}) collective-permute-start(bf16[128,576]{0,1:T(8,128)(2,1)} %param.9), channel_id=1, source_target_pairs={{0,24},{8,32},{16,40},{24,48},{32,56},{40,64},{48,72},{56,80},{64,... | collective-permute-start | bytes 442376 | tf_op jit(solution)/shard_map/ppermute | solution.py:15
  42.0 2.3 collective-permute-done.9
  44.3 6.2 %collective-permute-start.10 = (bf16[128,576]{0,1:T(8,128)(2,1)S(1)}, bf16[128,576]{0,1:T(8,128)(2,1)S(1)}, u32[]{:S(2)}, u32[]{:S(2)}) collective-permute-start(bf16[128,576]{0,1:T(8,128)(2,1)S(1)} %copy-done.2), channel_id=1, source_target_pairs={{0,32},{8,40},{16,48},{24,56},{32,64},{40,72},{48,80},{56,88},{64,... | collective-permute-start | bytes 442376 | tf_op jit(solution)/shard_map/ppermute | solution.py:15
  53.2 4.5 %collective-permute-start.11 = (bf16[128,576]{0,1:T(8,128)(2,1)S(1)}, bf16[128,576]{0,1:T(8,128)(2,1)S(1)}, u32[]{:S(2)}, u32[]{:S(2)}) collective-permute-start(bf16[128,576]{0,1:T(8,128)(2,1)S(1)} %copy-done.2), channel_id=1, source_target_pairs={{0,40},{8,48},{16,56},{24,64},{32,72},{40,80},{48,88},{56,96},{64,... | collective-permute-start | bytes 442376 | tf_op jit(solution)/shard_map/ppermute | solution.py:15
  58.4 2.8 %collective-permute-done.11 = bf16[128,576]{0,1:T(8,128)(2,1)S(1)} collective-permute-done((bf16[128,576]{0,1:T(8,128)(2,1)S(1)}, bf16[128,576]{0,1:T(8,128)(2,1)S(1)}, u32[]{:S(2)}, u32[]{:S(2)}) %collective-permute-start.11) | collective-permute-done | bytes 147488 | tf_op jit(solution)/shard_map/ppermute | solution.py:15
  61.1 15.5 %collective-permute-start.12 = (bf16[128,576]{0,1:T(8,128)(2,1)S(1)}, bf16[128,576]{0,1:T(8,128)(2,1)S(1)}, u32[]{:S(2)}, u32[]{:S(2)}) collective-permute-start(bf16[128,576]{0,1:T(8,128)(2,1)S(1)} %copy-done.2), channel_id=1, source_target_pairs={{0,48},{8,56},{16,64},{24,72},{32,80},{40,88},{48,96},{56,104},{64... | collective-permute-start | bytes 442376 | tf_op jit(solution)/shard_map/ppermute | solution.py:15
  77.3 2.7 %collective-permute-done.12 = bf16[128,576]{0,1:T(8,128)(2,1)S(1)} collective-permute-done((bf16[128,576]{0,1:T(8,128)(2,1)S(1)}, bf16[128,576]{0,1:T(8,128)(2,1)S(1)}, u32[]{:S(2)}, u32[]{:S(2)}) %collective-permute-start.12) | collective-permute-done | bytes 147488 | tf_op jit(solution)/shard_map/ppermute | solution.py:15
  80.1 7.1 %collective-permute-start.13 = (bf16[128,576]{0,1:T(8,128)(2,1)S(1)}, bf16[128,576]{0,1:T(8,128)(2,1)S(1)}, u32[]{:S(2)}, u32[]{:S(2)}) collective-permute-start(bf16[128,576]{0,1:T(8,128)(2,1)S(1)} %copy-done.2), channel_id=1, source_target_pairs={{0,56},{8,64},{16,72},{24,80},{32,88},{40,96},{48,104},{56,112},{6... | collective-permute-start | bytes 442376 | tf_op jit(solution)/shard_map/ppermute | solution.py:15
  92.5 2.0 copy.20
  95.9 7.9 %fusion.5 = f32[128,8,1024]{0,2,1:T(8,128)} fusion(pred[128,1024]{0,1:T(8,128)(4,1)} %and_and_fusion, bf16[1024,576,1]{0,1,2:T(8,128)(2,1)} %reshape.168, bf16[128,8,576]{0,2,1:T(8,128)(2,1)S(1)} %copy-done), kind=kOutput, calls=%fused_computation.7 | convolution fusion | flops 2421164032 | bytes 6684672 | tf_op jit(solution)/shard_map/sub | solution.py:25
  103.7 7.3 %fusion = f32[128,8,1024]{0,2,1:T(8,128)} fusion(pred[128,1024]{0,1:T(8,128)(4,1)} %and_and_fusion, bf16[1024,576,1]{0,1,2:T(8,128)(2,1)S(1)} %copy-done.1, bf16[128,8,576]{0,2,1:T(8,128)(2,1)S(1)} %copy-done), kind=kOutput, calls=%fused_computation | convolution fusion | flops 2421166080 | bytes 6684672 | tf_op jit(solution)/shard_map/div | solution.py:26
  111.1 7.4 %collective-permute-start.6 = (bf16[128,576]{0,1:T(8,128)(2,1)}, bf16[128,576]{0,1:T(8,128)(2,1)S(1)}, u32[]{:S(2)}, u32[]{:S(2)}) collective-permute-start(bf16[128,576]{0,1:T(8,128)(2,1)} %param.8), channel_id=1, source_target_pairs={{0,56},{8,64},{16,72},{24,80},{32,88},{40,96},{48,104},{56,112},{6... | collective-permute-start | bytes 442376 | tf_op jit(solution)/shard_map/ppermute | solution.py:15
  119.5 5.0 %collective-permute-start.5 = (bf16[128,576]{0,1:T(8,128)(2,1)}, bf16[128,576]{0,1:T(8,128)(2,1)S(1)}, u32[]{:S(2)}, u32[]{:S(2)}) collective-permute-start(bf16[128,576]{0,1:T(8,128)(2,1)} %param.8), channel_id=1, source_target_pairs={{0,48},{8,56},{16,64},{24,72},{32,80},{40,88},{48,96},{56,104},{64... | collective-permute-start | bytes 442376 | tf_op jit(solution)/shard_map/ppermute | solution.py:15
  130.7 10.6 %multiply_convert_fusion = bf16[128,8,1024]{0,2,1:T(8,128)(2,1)} fusion(f32[128,8,1024]{0,2,1:T(8,128)} %fusion.5, f32[128,8,1024]{0,2,1:T(8,128)} %fusion, f32[128,8]{0,1:T(8,128)S(1)} %copy-done.4, pred[128,1024]{0,1:T(8,128)(4,1)} %and_and_fusion, bf16[1024,576,1]{0,1,2:T(8,128)(2,1)S(1)} %reshape.167, bf16[128,8,576]{0,2,1:T(8,128)(2,1)} %param.6), kind=kOutput, calls=%fused_computation.12 | convolution fusion | flops 2427457536 | bytes 12980224 | tf_op jit(solution)/shard_map/div | solution.py:26
  141.2 3.0 %convolution_bitcast_fusion = f32[1024,576]{0,1:T(8,128)S(1)} fusion(bf16[128,8,1024]{0,2,1:T(8,128)(2,1)} %multiply_convert_fusion, bf16[128,8,576]{0,2,1:T(8,128)(2,1)S(1)} %copy-done.3), kind=kOutput, calls=%fused_computation.23 | convolution fusion | flops 1207959552 | bytes 5636096 | tf_op jit(solution)/shard_map/thk,thc->kc/dot_general | solution.py:72
  144.4 5.3 %collective-permute-start.14 = (f32[128,576]{0,1:T(8,128)S(1)}, f32[128,576]{0,1:T(8,128)S(1)}, u32[]{:S(2)}, u32[]{:S(2)}) collective-permute-start(f32[128,576]{0,1:T(8,128)S(1)} %get-tuple-element.2), channel_id=1, source_target_pairs={{8,0},{16,8},{24,16},{32,24},{40,32},{48,40},{56,48},{64,56},{72,6... | collective-permute-start | bytes 884744 | tf_op jit(solution)/shard_map/ppermute | solution.py:15
  149.7 3.6 %collective-permute-start.20 = (f32[128,576]{0,1:T(8,128)S(1)}, f32[128,576]{0,1:T(8,128)S(1)}, u32[]{:S(2)}, u32[]{:S(2)}) collective-permute-start(f32[128,576]{0,1:T(8,128)S(1)} %get-tuple-element.3), channel_id=1, source_target_pairs={{56,0},{64,8},{72,16},{80,24},{88,32},{96,40},{104,48},{112,56},{1... | collective-permute-start | bytes 884744 | tf_op jit(solution)/shard_map/ppermute | solution.py:15
  159.2 10.4 %collective-permute-start.16 = (f32[128,576]{0,1:T(8,128)S(1)}, f32[128,576]{0,1:T(8,128)S(1)}, u32[]{:S(2)}, u32[]{:S(2)}) collective-permute-start(f32[128,576]{0,1:T(8,128)S(1)} %get-tuple-element.7), channel_id=1, source_target_pairs={{24,0},{32,8},{40,16},{48,24},{56,32},{64,40},{72,48},{80,56},{88,... | collective-permute-start | bytes 884744 | tf_op jit(solution)/shard_map/ppermute | solution.py:15
  169.6 2.5 %collective-permute-done.20 = f32[128,576]{0,1:T(8,128)S(1)} collective-permute-done((f32[128,576]{0,1:T(8,128)S(1)}, f32[128,576]{0,1:T(8,128)S(1)}, u32[]{:S(2)}, u32[]{:S(2)}) %collective-permute-start.20) | collective-permute-done | bytes 294944 | tf_op jit(solution)/shard_map/ppermute | solution.py:15
  172.1 5.6 %collective-permute-start.15 = (f32[128,576]{0,1:T(8,128)S(1)}, f32[128,576]{0,1:T(8,128)S(1)}, u32[]{:S(2)}, u32[]{:S(2)}) collective-permute-start(f32[128,576]{0,1:T(8,128)S(1)} %get-tuple-element.8), channel_id=1, source_target_pairs={{16,0},{24,8},{32,16},{40,24},{48,32},{56,40},{64,48},{72,56},{80,... | collective-permute-start | bytes 884744 | tf_op jit(solution)/shard_map/ppermute | solution.py:15
  177.7 2.4 %convolution_convert_fusion = bf16[128,8,576]{0,2,1:T(8,128)(2,1)} fusion(bf16[1024,576,1]{0,1,2:T(8,128)(2,1)S(1)} %reshape.167, bf16[128,8,1024]{0,2,1:T(8,128)(2,1)S(1)} %copy-done.5), kind=kOutput, calls=%fused_computation.24 | convolution fusion | flops 1208549376 | bytes 4456448 | tf_op jit(solution)/shard_map/thk,kc->thc/dot_general | solution.py:69
  180.1 4.1 %collective-permute-done.19 = f32[128,576]{0,1:T(8,128)S(1)} collective-permute-done((f32[128,576]{0,1:T(8,128)S(1)}, f32[128,576]{0,1:T(8,128)S(1)}, u32[]{:S(2)}, u32[]{:S(2)}) %collective-permute-start.19) | collective-permute-done | bytes 294944 | tf_op jit(solution)/shard_map/ppermute | solution.py:15
  184.2 9.5 %collective-permute-done.16 = f32[128,576]{0,1:T(8,128)S(1)} collective-permute-done((f32[128,576]{0,1:T(8,128)S(1)}, f32[128,576]{0,1:T(8,128)S(1)}, u32[]{:S(2)}, u32[]{:S(2)}) %collective-permute-start.16) | collective-permute-done | bytes 294944 | tf_op jit(solution)/shard_map/ppermute | solution.py:15
  193.7 17.1 %collective-permute-done.15 = f32[128,576]{0,1:T(8,128)S(1)} collective-permute-done((f32[128,576]{0,1:T(8,128)S(1)}, f32[128,576]{0,1:T(8,128)S(1)}, u32[]{:S(2)}, u32[]{:S(2)}) %collective-permute-start.15) | collective-permute-done | bytes 294944 | tf_op jit(solution)/shard_map/ppermute | solution.py:15
  210.9 27.0 %all-reduce.1 = bf16[128,576]{0,1:T(8,128)(2,1)} all-reduce(f32[128,576]{0,1:T(8,128)S(1)} %fusion.23), channel_id=1, replica_groups=mesh['seq'=64,'head'=8] {'head'}, use_global_device_ids=true, to_apply=%region_7.8 | all-reduce | flops 73728 | bytes 442368 | tf_op jit(solution)/shard_map/psum | solution.py:79
  (60 shorter events, 30.3 us)
Async XLA Ops:
  0.6 95.2 %copy-start = (bf16[128,8,576]{0,2,1:T(8,128)(2,1)S(1)}, bf16[128,8,576]{0,2,1:T(8,128)(2,1)}, u32[]{:S(2)}) copy-start(bf16[128,8,576]{0,2,1:T(8,128)(2,1)} %param.7) | copy-start | bytes 3538948
  0.6 43.7 %copy-start.2 = (bf16[128,576]{0,1:T(8,128)(2,1)S(1)}, bf16[128,576]{0,1:T(8,128)(2,1)}, u32[]{:S(2)}) copy-start(bf16[128,576]{0,1:T(8,128)(2,1)} %param.9) | copy-start | bytes 442372
  0.7 126.7 %collective-permute-start.4 = (bf16[128,576]{0,1:T(8,128)(2,1)}, bf16[128,576]{0,1:T(8,128)(2,1)}, u32[]{:S(2)}, u32[]{:S(2)}) collective-permute-start(bf16[128,576]{0,1:T(8,128)(2,1)} %param.8), channel_id=1, source_target_pairs={{0,40},{8,48},{16,56},{24,64},{32,72},{40,80},{48,88},{56,96},{64,... | collective-permute-start | bytes 442376 | tf_op jit(solution)/shard_map/ppermute | solution.py:15
  5.3 121.0 %collective-permute-start.3 = (bf16[128,576]{0,1:T(8,128)(2,1)}, bf16[128,576]{0,1:T(8,128)(2,1)}, u32[]{:S(2)}, u32[]{:S(2)}) collective-permute-start(bf16[128,576]{0,1:T(8,128)(2,1)} %param.8), channel_id=1, source_target_pairs={{0,32},{8,40},{16,48},{24,56},{32,64},{40,72},{48,80},{56,88},{64,... | collective-permute-start | bytes 442376 | tf_op jit(solution)/shard_map/ppermute | solution.py:15
  10.4 115.0 %collective-permute-start.2 = (bf16[128,576]{0,1:T(8,128)(2,1)}, bf16[128,576]{0,1:T(8,128)(2,1)}, u32[]{:S(2)}, u32[]{:S(2)}) collective-permute-start(bf16[128,576]{0,1:T(8,128)(2,1)} %param.8), channel_id=1, source_target_pairs={{0,24},{8,32},{16,40},{24,48},{32,56},{40,64},{48,72},{56,80},{64,... | collective-permute-start | bytes 442376 | tf_op jit(solution)/shard_map/ppermute | solution.py:15
  14.4 105.1 %collective-permute-start.1 = (bf16[128,576]{0,1:T(8,128)(2,1)}, bf16[128,576]{0,1:T(8,128)(2,1)}, u32[]{:S(2)}, u32[]{:S(2)}) collective-permute-start(bf16[128,576]{0,1:T(8,128)(2,1)} %param.8), channel_id=1, source_target_pairs={{0,16},{8,24},{16,32},{24,40},{32,48},{40,56},{48,64},{56,72},{64,... | collective-permute-start | bytes 442376 | tf_op jit(solution)/shard_map/ppermute | solution.py:15
  19.2 8.1 %collective-permute-start.7 = (bf16[128,576]{0,1:T(8,128)(2,1)}, bf16[128,576]{0,1:T(8,128)(2,1)S(1)}, u32[]{:S(2)}, u32[]{:S(2)}) collective-permute-start(bf16[128,576]{0,1:T(8,128)(2,1)} %param.9), channel_id=1, source_target_pairs={{0,8},{8,16},{16,24},{24,32},{32,40},{40,48},{48,56},{56,64},{64,7... | collective-permute-start | bytes 442376 | tf_op jit(solution)/shard_map/ppermute | solution.py:15
  27.4 8.7 %collective-permute-start.8 = (bf16[128,576]{0,1:T(8,128)(2,1)}, bf16[128,576]{0,1:T(8,128)(2,1)S(1)}, u32[]{:S(2)}, u32[]{:S(2)}) collective-permute-start(bf16[128,576]{0,1:T(8,128)(2,1)} %param.9), channel_id=1, source_target_pairs={{0,16},{8,24},{16,32},{24,40},{32,48},{40,56},{48,64},{56,72},{64,... | collective-permute-start | bytes 442376 | tf_op jit(solution)/shard_map/ppermute | solution.py:15
  36.1 8.2 %collective-permute-start.9 = (bf16[128,576]{0,1:T(8,128)(2,1)}, bf16[128,576]{0,1:T(8,128)(2,1)S(1)}, u32[]{:S(2)}, u32[]{:S(2)}) collective-permute-start(bf16[128,576]{0,1:T(8,128)(2,1)} %param.9), channel_id=1, source_target_pairs={{0,24},{8,32},{16,40},{24,48},{32,56},{40,64},{48,72},{56,80},{64,... | collective-permute-start | bytes 442376 | tf_op jit(solution)/shard_map/ppermute | solution.py:15
  44.3 8.9 %collective-permute-start.10 = (bf16[128,576]{0,1:T(8,128)(2,1)S(1)}, bf16[128,576]{0,1:T(8,128)(2,1)S(1)}, u32[]{:S(2)}, u32[]{:S(2)}) collective-permute-start(bf16[128,576]{0,1:T(8,128)(2,1)S(1)} %copy-done.2), channel_id=1, source_target_pairs={{0,32},{8,40},{16,48},{24,56},{32,64},{40,72},{48,80},{56,88},{64,... | collective-permute-start | bytes 442376 | tf_op jit(solution)/shard_map/ppermute | solution.py:15
  53.2 7.9 %collective-permute-start.11 = (bf16[128,576]{0,1:T(8,128)(2,1)S(1)}, bf16[128,576]{0,1:T(8,128)(2,1)S(1)}, u32[]{:S(2)}, u32[]{:S(2)}) collective-permute-start(bf16[128,576]{0,1:T(8,128)(2,1)S(1)} %copy-done.2), channel_id=1, source_target_pairs={{0,40},{8,48},{16,56},{24,64},{32,72},{40,80},{48,88},{56,96},{64,... | collective-permute-start | bytes 442376 | tf_op jit(solution)/shard_map/ppermute | solution.py:15
  61.1 19.0 %collective-permute-start.12 = (bf16[128,576]{0,1:T(8,128)(2,1)S(1)}, bf16[128,576]{0,1:T(8,128)(2,1)S(1)}, u32[]{:S(2)}, u32[]{:S(2)}) collective-permute-start(bf16[128,576]{0,1:T(8,128)(2,1)S(1)} %copy-done.2), channel_id=1, source_target_pairs={{0,48},{8,56},{16,64},{24,72},{32,80},{40,88},{48,96},{56,104},{64... | collective-permute-start | bytes 442376 | tf_op jit(solution)/shard_map/ppermute | solution.py:15
  80.1 9.8 %collective-permute-start.13 = (bf16[128,576]{0,1:T(8,128)(2,1)S(1)}, bf16[128,576]{0,1:T(8,128)(2,1)S(1)}, u32[]{:S(2)}, u32[]{:S(2)}) collective-permute-start(bf16[128,576]{0,1:T(8,128)(2,1)S(1)} %copy-done.2), channel_id=1, source_target_pairs={{0,56},{8,64},{16,72},{24,80},{32,88},{40,96},{48,104},{56,112},{6... | collective-permute-start | bytes 442376 | tf_op jit(solution)/shard_map/ppermute | solution.py:15
  89.9 21.2 %collective-permute-start = (bf16[128,576]{0,1:T(8,128)(2,1)}, bf16[128,576]{0,1:T(8,128)(2,1)}, u32[]{:S(2)}, u32[]{:S(2)}) collective-permute-start(bf16[128,576]{0,1:T(8,128)(2,1)} %param.8), channel_id=1, source_target_pairs={{0,8},{8,16},{16,24},{24,32},{32,40},{40,48},{48,56},{56,64},{64,7... | collective-permute-start | bytes 442376 | tf_op jit(solution)/shard_map/ppermute | solution.py:15
  95.9 7.9 %copy-start.1 = (bf16[1024,576,1]{0,1,2:T(8,128)(2,1)S(1)}, bf16[1024,576,1]{0,1,2:T(8,128)(2,1)}, u32[]{:S(2)}) copy-start(bf16[1024,576,1]{0,1,2:T(8,128)(2,1)} %reshape.168) | copy-start | bytes 3538948
  111.1 18.1 %collective-permute-start.6 = (bf16[128,576]{0,1:T(8,128)(2,1)}, bf16[128,576]{0,1:T(8,128)(2,1)S(1)}, u32[]{:S(2)}, u32[]{:S(2)}) collective-permute-start(bf16[128,576]{0,1:T(8,128)(2,1)} %param.8), channel_id=1, source_target_pairs={{0,56},{8,64},{16,72},{24,80},{32,88},{40,96},{48,104},{56,112},{6... | collective-permute-start | bytes 442376 | tf_op jit(solution)/shard_map/ppermute | solution.py:15
  119.5 9.7 %collective-permute-start.5 = (bf16[128,576]{0,1:T(8,128)(2,1)}, bf16[128,576]{0,1:T(8,128)(2,1)S(1)}, u32[]{:S(2)}, u32[]{:S(2)}) collective-permute-start(bf16[128,576]{0,1:T(8,128)(2,1)} %param.8), channel_id=1, source_target_pairs={{0,48},{8,56},{16,64},{24,72},{32,80},{40,88},{48,96},{56,104},{64... | collective-permute-start | bytes 442376 | tf_op jit(solution)/shard_map/ppermute | solution.py:15
  130.0 0.7 copy-start.4
  130.6 10.6 %copy-start.3 = (bf16[128,8,576]{0,2,1:T(8,128)(2,1)S(1)}, bf16[128,8,576]{0,2,1:T(8,128)(2,1)}, u32[]{:S(2)}) copy-start(bf16[128,8,576]{0,2,1:T(8,128)(2,1)} %param.6) | copy-start | bytes 3538948
  144.3 33.4 %copy-start.5 = (bf16[128,8,1024]{0,2,1:T(8,128)(2,1)S(1)}, bf16[128,8,1024]{0,2,1:T(8,128)(2,1)}, u32[]{:S(2)}) copy-start(bf16[128,8,1024]{0,2,1:T(8,128)(2,1)} %multiply_convert_fusion) | copy-start | bytes 6291460
  144.4 14.8 %collective-permute-start.14 = (f32[128,576]{0,1:T(8,128)S(1)}, f32[128,576]{0,1:T(8,128)S(1)}, u32[]{:S(2)}, u32[]{:S(2)}) collective-permute-start(f32[128,576]{0,1:T(8,128)S(1)} %get-tuple-element.2), channel_id=1, source_target_pairs={{8,0},{16,8},{24,16},{32,24},{40,32},{48,40},{56,48},{64,56},{72,6... | collective-permute-start | bytes 884744 | tf_op jit(solution)/shard_map/ppermute | solution.py:15
  149.7 22.4 %collective-permute-start.20 = (f32[128,576]{0,1:T(8,128)S(1)}, f32[128,576]{0,1:T(8,128)S(1)}, u32[]{:S(2)}, u32[]{:S(2)}) collective-permute-start(f32[128,576]{0,1:T(8,128)S(1)} %get-tuple-element.3), channel_id=1, source_target_pairs={{56,0},{64,8},{72,16},{80,24},{88,32},{96,40},{104,48},{112,56},{1... | collective-permute-start | bytes 884744 | tf_op jit(solution)/shard_map/ppermute | solution.py:15
  153.4 30.8 %collective-permute-start.19 = (f32[128,576]{0,1:T(8,128)S(1)}, f32[128,576]{0,1:T(8,128)S(1)}, u32[]{:S(2)}, u32[]{:S(2)}) collective-permute-start(f32[128,576]{0,1:T(8,128)S(1)} %get-tuple-element.4), channel_id=1, source_target_pairs={{48,0},{56,8},{64,16},{72,24},{80,32},{88,40},{96,48},{104,56},{11... | collective-permute-start | bytes 884744 | tf_op jit(solution)/shard_map/ppermute | solution.py:15
  155.3 28.9 %collective-permute-start.18 = (f32[128,576]{0,1:T(8,128)S(1)}, f32[128,576]{0,1:T(8,128)S(1)}, u32[]{:S(2)}, u32[]{:S(2)}) collective-permute-start(f32[128,576]{0,1:T(8,128)S(1)} %get-tuple-element.5), channel_id=1, source_target_pairs={{40,0},{48,8},{56,16},{64,24},{72,32},{80,40},{88,48},{96,56},{104... | collective-permute-start | bytes 884744 | tf_op jit(solution)/shard_map/ppermute | solution.py:15
  157.2 27.0 %collective-permute-start.17 = (f32[128,576]{0,1:T(8,128)S(1)}, f32[128,576]{0,1:T(8,128)S(1)}, u32[]{:S(2)}, u32[]{:S(2)}) collective-permute-start(f32[128,576]{0,1:T(8,128)S(1)} %get-tuple-element.6), channel_id=1, source_target_pairs={{32,0},{40,8},{48,16},{56,24},{64,32},{72,40},{80,48},{88,56},{96,... | collective-permute-start | bytes 884744 | tf_op jit(solution)/shard_map/ppermute | solution.py:15
  159.2 34.5 %collective-permute-start.16 = (f32[128,576]{0,1:T(8,128)S(1)}, f32[128,576]{0,1:T(8,128)S(1)}, u32[]{:S(2)}, u32[]{:S(2)}) collective-permute-start(f32[128,576]{0,1:T(8,128)S(1)} %get-tuple-element.7), channel_id=1, source_target_pairs={{24,0},{32,8},{40,16},{48,24},{56,32},{64,40},{72,48},{80,56},{88,... | collective-permute-start | bytes 884744 | tf_op jit(solution)/shard_map/ppermute | solution.py:15
  172.1 38.7 %collective-permute-start.15 = (f32[128,576]{0,1:T(8,128)S(1)}, f32[128,576]{0,1:T(8,128)S(1)}, u32[]{:S(2)}, u32[]{:S(2)}) collective-permute-start(f32[128,576]{0,1:T(8,128)S(1)} %get-tuple-element.8), channel_id=1, source_target_pairs={{16,0},{24,8},{32,16},{40,24},{48,32},{56,40},{64,48},{72,56},{80,... | collective-permute-start | bytes 884744 | tf_op jit(solution)/shard_map/ppermute | solution.py:15
where the time goes:
time: 239 us; the launch traced here: 238 us
  starting transfers between devices  110 us (46%)
  waiting for transfers between devices  48.8 us (20%)
  matrix products  31.2 us (13%)
  blocking collectives  27 us (11%)
  local copies, waits for them, and re-layouts  17.6 us (7%)
    ppermute x21, starting transfers between devices, from_behind(): return lax.ppermute(block, axis, route)  110 us
    ppermute x21, waiting for transfers between devices, from_behind(): return lax.ppermute(block, axis, route)  48.8 us
    psum x1, blocking collectives, on_device(): key_grad = lax.psum(summed, 'head').astype(jnp.bfloat16)  27 us
    div x2, matrix products, masked_softmax(): return expo / jnp.sum(expo, axis=-1, keepdims=True)  17.9 us
    unnamed x26, local copies, waits for them, and re-layouts  11.4 us
    sub x1, matrix products, masked_softmax(): expo = jnp.where(visible, jnp.exp(scores - peak), 0.0)  7.86 us
  transfers between devices with their start and end apart: 21, of which 12 were waited for; matrix products, arithmetic and copies ran while one was open for 15% of the time, Pallas kernels for 0%

commit v1 on v0

v1 whole, which is shorter than its diff:
```python
import math

import jax
import jax.numpy as jnp
from jax import lax
from jax.experimental import pallas as pl
from jax.experimental.pallas import tpu as pltpu
from jax.sharding import Mesh
from jax.sharding import PartitionSpec as P

SEQ_GROUP = 8
TOK = 128
WIN = SEQ_GROUP * TOK
KDIM = 576
HALF = KDIM // 2
PIECE = KDIM // 4
HEADS = 8
SCALE = 192.0 ** (-0.5)
SCALE_LOG2 = SCALE * math.log2(math.e)
HIDDEN = -1e30
VMEM = 48 * 1024 * 1024


def key_rows(kt_ref, k_ref):
    for j in range(SEQ_GROUP):
        k_ref[j * TOK : (j + 1) * TOK, :] = kt_ref[j].T


def hidden_bias(meta, bias_ref):
    me, seq = meta[1], meta[2]
    query_pos = seq * TOK + lax.broadcasted_iota(jnp.int32, (1, TOK), 1)
    start = jnp.zeros((1, TOK), jnp.int32)
    end = jnp.int32(0)
    for m in range(16):
        end = end + meta[3 + m]
        start = jnp.where(query_pos >= end, end, start)
    row = lax.broadcasted_iota(jnp.int32, (TOK, TOK), 0)
    for j in range(SEQ_GROUP):
        block = seq - me + j - jnp.where(j > me, SEQ_GROUP, 0)
        key_pos = block * TOK + row
        seen = (key_pos >= start) & (key_pos <= query_pos)
        bias_ref[j * TOK : (j + 1) * TOK, :] = jnp.where(seen, 0.0, HIDDEN)


def both(a, b):
    return jnp.concatenate([a, b], axis=1)


def exponentials(k_ref, bias_ref, queries, s_ref):
    s_ref[...] = jnp.dot(k_ref[...], queries, preferred_element_type=jnp.float32)
    peak = jnp.full((8, 2 * TOK), HIDDEN, jnp.float32)
    for j in range(SEQ_GROUP):
        rows = slice(j * TOK, (j + 1) * TOK)
        bias = bias_ref[rows, :]
        s = s_ref[rows, :] + both(bias, bias)
        s_ref[rows, :] = s
        peak = jnp.maximum(peak, jnp.max(s.reshape(TOK // 8, 8, 2 * TOK), axis=0))
    peak = jnp.max(peak, axis=0, keepdims=True)
    total = jnp.zeros((8, 2 * TOK), jnp.float32)
    for j in range(SEQ_GROUP):
        rows = slice(j * TOK, (j + 1) * TOK)
        e = jnp.exp2((s_ref[rows, :] - peak) * SCALE_LOG2)
        s_ref[rows, :] = e
        total = total + jnp.sum(e.reshape(TOK // 8, 8, 2 * TOK), axis=0)
    return jnp.sum(total, axis=0, keepdims=True)


def pair_weight(lw_ref, i):
    return both(lw_ref[pl.ds(2 * i, 1), :], lw_ref[pl.ds(2 * i + 1, 1), :]) * SCALE


def first_kernel(meta, kt_ref, sq_ref, tq_ref, lw_ref, p_ref, k_ref, bias_ref, s_ref):
    i = pl.program_id(0)
    core = meta[0]

    @pl.when(i == 0)
    def _():
        key_rows(kt_ref, k_ref)
        hidden_bias(meta, bias_ref)

    student = core == 0
    queries = both(
        jnp.where(student, sq_ref[0], tq_ref[0]), jnp.where(student, sq_ref[1], tq_ref[1])
    )
    total = exponentials(k_ref, bias_ref, queries, s_ref)
    factor = pair_weight(lw_ref, i) / total
    for j in range(SEQ_GROUP):
        rows = slice(j * TOK, (j + 1) * TOK)
        p_ref[rows, :] = s_ref[rows, :] * factor


def second_kernel(
    meta, kt_ref, sq_ref, tq_ref, lw_ref, p_ref, sh_ref, g_ref, kg_ref, k_ref, bias_ref, s_ref, all_ref
):
    i = pl.program_id(0)
    core = meta[0]

    @pl.when(i == 0)
    def _():
        key_rows(kt_ref, k_ref)
        hidden_bias(meta, bias_ref)

    student = core == 1
    queries = both(
        jnp.where(student, sq_ref[0], tq_ref[0]), jnp.where(student, sq_ref[1], tq_ref[1])
    )
    total = exponentials(k_ref, bias_ref, queries, s_ref)
    factor = pair_weight(lw_ref, i) / total
    sign = jnp.where(student, -1.0, 1.0)
    lanes = pl.ds(pl.multiple_of(i * 2 * TOK, 2 * TOK), 2 * TOK)
    for j in range(SEQ_GROUP):
        rows = slice(j * TOK, (j + 1) * TOK)
        g = ((p_ref[rows, :] - s_ref[rows, :] * factor) * sign).astype(jnp.bfloat16)
        g_ref[rows, :] = g
        all_ref[rows, lanes] = g

    @pl.when(i == HEADS // 2 - 1)
    def _():
        half = jnp.concatenate([sh_ref[h] for h in range(HEADS)], axis=1)
        for j in range(SEQ_GROUP // 2):
            grad = lax.dot_general(
                half,
                all_ref[j * 2 * TOK : (j + 1) * 2 * TOK, :],
                (((1,), (1,)), ((), ())),
                preferred_element_type=jnp.float32,
            ).astype(jnp.bfloat16)
            kg_ref[2 * j] = grad[:, :TOK]
            kg_ref[2 * j + 1] = grad[:, TOK:]


def query_kernel(meta, mine_ref, other_ref, g_ref, out_ref, kt_ref):
    @pl.when(pl.program_id(0) == 0)
    def _():
        @pl.when(meta[0] == 0)
        def _():
            for j in range(SEQ_GROUP):
                kt_ref[:, j * TOK : (j + 1) * TOK] = mine_ref[j]

        @pl.when(meta[0] == 1)
        def _():
            for j in range(SEQ_GROUP):
                kt_ref[:, j * TOK : (j + 1) * TOK] = other_ref[j]

    grad = jnp.dot(kt_ref[...], g_ref[...], preferred_element_type=jnp.float32).astype(jnp.bfloat16)
    out_ref[0] = grad[:, :TOK]
    out_ref[1] = grad[:, TOK:]


def key_kernel(meta, sh_ref, g_ref, got_ref, out_ref):
    half = jnp.concatenate([sh_ref[h] for h in range(HEADS)], axis=1)
    grad = lax.dot_general(
        half, g_ref[...], (((1,), (1,)), ((), ())), preferred_element_type=jnp.float32
    )
    out_ref[0] = (grad[:, :TOK] + got_ref[0].astype(jnp.float32)).astype(jnp.bfloat16)
    out_ref[1] = (grad[:, TOK:] + got_ref[1].astype(jnp.float32)).astype(jnp.bfloat16)


def call(kernel, grid, in_specs, out_specs, out_shape, scratch, flops, args):
    return pl.pallas_call(
        kernel,
        grid_spec=pltpu.PrefetchScalarGridSpec(
            num_scalar_prefetch=1,
            grid=(grid,),
            in_specs=in_specs,
            out_specs=out_specs,
            scratch_shapes=scratch,
        ),
        out_shape=out_shape,
        compiler_params=pltpu.CompilerParams(vmem_limit_bytes=VMEM),
        cost_estimate=pl.CostEstimate(flops=flops, bytes_accessed=8 << 20, transcendentals=1 << 20),
    )(*args)


def on_device(student_query, teacher_query, student_keys, teacher_keys, loss_weight, doc_lengths):
    core = lax.axis_index("c")
    x = lax.axis_index("x")
    me = lax.axis_index(("zi", "y"))
    seq = lax.axis_index(("zo", "zi", "y"))
    meta = jnp.concatenate([jnp.stack([core, me, seq]).astype(jnp.int32), doc_lengths])
    sq = student_query.transpose(1, 2, 0)
    tq = teacher_query.transpose(1, 2, 0)
    lw = loss_weight.T

    table = jnp.where(core == 0, student_keys.T, teacher_keys.T)
    own = lax.dynamic_slice_in_dim(table, x * PIECE, PIECE, 0)
    before = lax.ppermute(own, ("zo", "zi"), [(i, (i + 2) % 16) for i in range(16)])
    later = (jnp.arange(SEQ_GROUP) >= me)[:, None, None, None]
    outgoing = jnp.broadcast_to(jnp.where(later, own, before), (SEQ_GROUP, 4, PIECE, TOK))
    mine = lax.all_to_all(
        outgoing.reshape(SEQ_GROUP * 4, PIECE, TOK), ("zi", "y", "x"), 0, 0, tiled=True
    ).reshape(SEQ_GROUP, KDIM, TOK)
    other = lax.ppermute(mine, "c", [(0, 1), (1, 0)])

    whole_keys = pl.BlockSpec((SEQ_GROUP, KDIM, TOK), lambda i, m: (0, 0, 0))
    on_first = pl.BlockSpec((2, KDIM, TOK), lambda i, m: (i * (1 - m[0]), 0, 0))
    on_second = pl.BlockSpec((2, KDIM, TOK), lambda i, m: (i * m[0], 0, 0))
    weights = pl.BlockSpec((HEADS, TOK), lambda i, m: (0, 0))
    pair = pl.BlockSpec((WIN, 2 * TOK), lambda i, m: (0, i))
    scratch = [
        pltpu.VMEM((WIN, KDIM), jnp.bfloat16),
        pltpu.VMEM((WIN, TOK), jnp.float32),
        pltpu.VMEM((WIN, 2 * TOK), jnp.float32),
    ]
    matmul = 2 * WIN * HEADS * TOK * KDIM
    probs = call(
        first_kernel,
        HEADS // 2,
        [whole_keys, on_first, on_second, weights],
        pair,
        jax.ShapeDtypeStruct((WIN, HEADS * TOK), jnp.float32),
        scratch,
        matmul,
        (meta, mine, sq, tq, lw),
    )
    score_grad, sent = call(
        second_kernel,
        HEADS // 2,
        [
            whole_keys,
            on_second,
            on_first,
            weights,
            pair,
            pl.BlockSpec((HEADS, HALF, TOK), lambda i, m: (0, 1 - m[0], 0)),
        ],
        [pair, pl.BlockSpec((SEQ_GROUP, HALF, TOK), lambda i, m: (0, 0, 0))],
        [
            jax.ShapeDtypeStruct((WIN, HEADS * TOK), jnp.bfloat16),
            jax.ShapeDtypeStruct((SEQ_GROUP, HALF, TOK), jnp.bfloat16),
        ],
        scratch + [pltpu.VMEM((WIN, HEADS * TOK), jnp.bfloat16)],
        matmul * 3 // 2,
        (meta, other, sq, tq, lw, probs, sq),
    )
    got = lax.ppermute(sent, "c", [(0, 1), (1, 0)])
    query_grad = call(
        query_kernel,
        HEADS // 2,
        [whole_keys, whole_keys, pair],
        pl.BlockSpec((2, KDIM, TOK), lambda i, m: (i, 0, 0)),
        jax.ShapeDtypeStruct((HEADS, KDIM, TOK), jnp.bfloat16),
        [pltpu.VMEM((KDIM, WIN), jnp.bfloat16)],
        matmul,
        (meta, mine, other, score_grad),
    )
    two_blocks = pl.BlockSpec((2, HALF, TOK), lambda i, m: (i, 0, 0))
    partial = call(
        key_kernel,
        SEQ_GROUP // 2,
        [
            pl.BlockSpec((HEADS, HALF, TOK), lambda i, m: (0, m[0], 0)),
            pl.BlockSpec((2 * TOK, HEADS * TOK), lambda i, m: (i, 0)),
            two_blocks,
        ],
        two_blocks,
        jax.ShapeDtypeStruct((SEQ_GROUP, HALF, TOK), jnp.bfloat16),
        [],
        matmul // 2,
        (meta, sq, score_grad, got),
    )
    rows = HALF // 4
    terms = lax.all_to_all(
        partial.reshape(SEQ_GROUP * 4, rows, TOK), ("zi", "y", "x"), 0, 0, tiled=True
    ).reshape(SEQ_GROUP, 4, rows, TOK)
    terms = jnp.sum(terms.astype(jnp.float32), axis=1)
    here = (jnp.arange(SEQ_GROUP) >= me)[:, None, None]
    kept = jnp.sum(jnp.where(here, terms, 0.0), axis=0)
    returned = jnp.sum(jnp.where(here, 0.0, terms), axis=0)
    returned = lax.ppermute(returned, ("zo", "zi"), [(i, (i - 2) % 16) for i in range(16)])
    share = (kept + returned).astype(jnp.bfloat16)
    key_grad = lax.all_to_all(
        jnp.broadcast_to(share, (8, rows, TOK)), ("c", "x"), 0, 0, tiled=True
    ).reshape(KDIM, TOK)
    return (query_grad.transpose(2, 0, 1), key_grad.T)


def solution(mesh):
    fine = Mesh(mesh.devices.reshape(8, 2, 4, 4, 2), ("zo", "zi", "y", "x", "c"))
    seq, head = ("zo", "zi", "y"), ("x", "c")
    return jax.shard_map(
        on_device,
        mesh=fine,
        in_specs=(
            P(seq, head, None),
            P(seq, head, None),
            P(seq, None),
            P(seq, None),
            P(seq, head),
            P(),
        ),
        out_specs=(P(seq, head, None), P(seq, None)),
        check_vma=False,
    )
```

time: 239 us -> 103 us (0.43)
  the two profiles are of different devices: /device:TPU:80 before, /device:TPU:1 now
where the time goes in v1:
time: 103 us; the launch traced here: 102 us
  blocking collectives  38.9 us (38%)
  starting transfers between devices  23.8 us (23%)
  Pallas kernels  21.5 us (21%)
  waiting for transfers between devices  11.2 us (11%)
  local copies, waits for them, and re-layouts  4.7 us (5%)
  other arithmetic  1.17 us (1%)
    all_to_all x1, blocking collectives, on_device(): lax.all_to_all(outgoing.reshape(SEQ_GROUP * 4, PIECE, TOK), ('zi', 'y', '...  24.5 us
    pallas_call x4, Pallas kernels, call(): pl.pallas_call(kernel, grid_spec=pltpu.PrefetchScalarGridSpec(num_scalar_...  21.5 us
    all_to_all x1, blocking collectives, on_device(): lax.all_to_all(partial.reshape(SEQ_GROUP * 4, rows, TOK), ('zi', 'y', 'x'...  14.4 us
    ppermute x1, waiting for transfers between devices, on_device(): lax.ppermute(own, ('zo', 'zi'), [(i, (i + 2) % 16) for i in range(16)])  7.98 us
    all_to_all x1, starting transfers between devices, on_device(): lax.all_to_all(jnp.broadcast_to(share, (8, rows, TOK)), ('c', 'x'), 0, 0,...  6.85 us
    ppermute x1, starting transfers between devices, on_device(): lax.ppermute(own, ('zo', 'zi'), [(i, (i + 2) % 16) for i in range(16)])  5.73 us
    ppermute x1, starting transfers between devices, on_device(): other = lax.ppermute(mine, 'c', [(0, 1), (1, 0)])  4.92 us
    ppermute x1, starting transfers between devices, on_device(): lax.ppermute(returned, ('zo', 'zi'), [(i, (i - 2) % 16) for i in range(16)])  4.34 us
  transfers between devices with their start and end apart: 5, of which 3 were waited for; matrix products, arithmetic and copies ran while one was open for 0% of the time, Pallas kernels for 11%

profile of v1, /device:TPU:1, one launch (start us, length us, event | category | flops | bytes accessed | tf_op | source)
XLA Modules:
  0.0 102.0 jit_solution(14967072917455273658)
XLA Ops:
  0.6 0.8 fusion
  1.4 5.7 %collective-permute-start = (bf16[144,128]{1,0:T(8,128)(2,1)S(1)}, bf16[144,128]{1,0:T(8,128)(2,1)S(1)}, u32[]{:S(2)}, u32[]{:S(2)}) collective-permute-start(bf16[144,128]{1,0:T(8,128)(2,1)S(1)} %fusion), channel_id=1, source_target_pairs={{0,64},{32,96},{64,128},{96,160},{128,192},{160,224},{192,256},{22... | collective-permute-start | bytes 110600 | tf_op jit(solution)/shard_map/ppermute | solution.py:186
  7.2 8.0 %collective-permute-done = bf16[144,128]{1,0:T(8,128)(2,1)S(1)} collective-permute-done((bf16[144,128]{1,0:T(8,128)(2,1)S(1)}, bf16[144,128]{1,0:T(8,128)(2,1)S(1)}, u32[]{:S(2)}, u32[]{:S(2)}) %collective-permute-start) | collective-permute-done | bytes 36896 | tf_op jit(solution)/shard_map/ppermute | solution.py:186
  15.2 0.1 broadcast_select_fusion
  15.3 0.2 broadcast_in_dim.49
  15.4 0.0 copy-start.5
  15.5 0.0 copy-start
  15.5 0.0 copy-start.3
  15.5 0.0 copy-start.4
  15.5 24.5 %all_to_all.15 = bf16[32,144,128]{2,1,0:T(8,128)(2,1)S(1)} all-to-all(bf16[32,144,128]{2,1,0:T(8,128)(2,1)S(1)} %bitcast.30), channel_id=1, replica_groups=mesh['zo'=8,'zi'=2,'y'=4,'x'=4,'c'=2] {'zi','y','x'}, dimensions={0} | all-to-all | bytes 2359296 | tf_op jit(solution)/shard_map/all_to_all | solution.py:189
  39.9 4.9 %collective-permute-start.1 = (bf16[8,576,128]{2,1,0:T(8,128)(2,1)S(1)}, bf16[8,576,128]{2,1,0:T(8,128)(2,1)}, u32[]{:S(2)}, u32[]{:S(2)}) collective-permute-start(bf16[8,576,128]{2,1,0:T(8,128)(2,1)S(1)} %bitcast.22), channel_id=1, source_target_pairs={{0,1},{1,0},{2,3},{3,2},{4,5},{5,4},{6,7},{7,6},{8,9},{9,8},{10,11... | collective-permute-start | bytes 3538952 | tf_op jit(solution)/shard_map/ppermute | solution.py:192
  44.9 0.0 copy-done.5
  44.9 0.1 pad_add_fusion.meta
  45.0 0.0 copy-done
  45.0 5.6 %shard_map.77.p_ref = f32[1024,1024]{1,0:T(8,128)} custom-call(s32[19]{0:T(128)S(1)} %pad_add_fusion.meta, bf16[8,576,128]{2,1,0:T(8,128)(2,1)S(1)} %bitcast.23, bf16[8,576,128]{2,1,0:T(8,128)(2,1)S(1)} %bitcast.18, bf16[8,576,128]{2,1,0:T(8,128)(2,1)S(1)} %bitcast.25, f32[8,128]{1,0:T(8,128)S(1)} %bitcast.28), custom_call_target="tpu_custom_call" | custom-call | flops 1207959552 | bytes 8388608 | tf_op jit(solution)/shard_map/pallas_call | solution.py:159
  50.6 0.0 collective-permute-done.1.kt_ref.other_ref
  50.6 8.6 %shard_map.78 = (bf16[1024,1024]{1,0:T(8,128)(2,1)}, bf16[8,288,128]{2,1,0:T(8,128)(2,1)S(1)}) custom-call(s32[19]{0:T(128)S(1)} %pad_add_fusion.meta, bf16[8,576,128]{2,1,0:T(8,128)(2,1)} %collective-permute-done.1.kt_ref.other_ref, bf16[8,576,128]{2,1,0:T(8,128)(2,1)S(1)} %bitcast.19, bf16[8,576,128]{2,1,0:T(8,128)(2,1)S(1)} %bitcast.26, ...), custom_call_target="tpu_custom_call" | custom-call | flops 1811939328 | bytes 8388608 | tf_op jit(solution)/shard_map/pallas_call | solution.py:159
  59.3 1.9 %collective-permute-start.2 = (bf16[8,288,128]{2,1,0:T(8,128)(2,1)S(1)}, bf16[8,288,128]{2,1,0:T(8,128)(2,1)S(1)}, u32[]{:S(2)}, u32[]{:S(2)}) collective-permute-start(bf16[8,288,128]{2,1,0:T(8,128)(2,1)S(1)} %get-tuple-element.5), channel_id=1, source_target_pairs={{0,1},{1,0},{2,3},{3,2},{4,5},{5,4},{6,7},{7,6},{8,9},{9,8},{10,11... | collective-permute-start | bytes 1769480 | tf_op jit(solution)/shard_map/ppermute | solution.py:235
  61.2 2.0 %collective-permute-done.2.got_ref = bf16[8,288,128]{2,1,0:T(8,128)(2,1)S(1)} collective-permute-done((bf16[8,288,128]{2,1,0:T(8,128)(2,1)S(1)}, bf16[8,288,128]{2,1,0:T(8,128)(2,1)S(1)}, u32[]{:S(2)}, u32[]{:S(2)}) %collective-permute-start.2) | collective-permute-done | bytes 589856 | tf_op jit(solution)/shard_map/ppermute | solution.py:235
  63.2 1.6 %copy-done.1 = bf16[1024,1024]{1,0:T(8,128)(2,1)S(1)} copy-done((bf16[1024,1024]{1,0:T(8,128)(2,1)S(1)}, bf16[1024,1024]{1,0:T(8,128)(2,1)}, u32[]{:S(2)}) %copy-start.1) | copy-done | bytes 2097176
  64.8 2.1 %shard_map.80 = bf16[8,288,128]{2,1,0:T(8,128)(2,1)S(1)} custom-call(s32[19]{0:T(128)S(1)} %pad_add_fusion.meta, bf16[8,576,128]{2,1,0:T(8,128)(2,1)S(1)} %bitcast.21, bf16[1024,1024]{1,0:T(8,128)(2,1)S(1)} %copy-done.1, bf16[8,288,128]{2,1,0:T(8,128)(2,1)S(1)} %collective-permute-done.2.got_ref), custom_call_target="tpu_custom_call" | custom-call | flops 603979776 | bytes 8388608 | tf_op jit(solution)/shard_map/pallas_call | solution.py:159
  66.8 14.4 %all_to_all.16 = bf16[32,72,128]{2,1,0:T(8,128)(2,1)S(1)} all-to-all(bf16[32,72,128]{2,1,0:T(8,128)(2,1)S(1)} %bitcast.27), channel_id=1, replica_groups=mesh['zo'=8,'zi'=2,'y'=4,'x'=4,'c'=2] {'zi','y','x'}, dimensions={0} | all-to-all | bytes 1179648 | tf_op jit(solution)/shard_map/all_to_all | solution.py:262
  81.2 0.1 convert_reduce_fusion
  81.3 0.1 select_reduce_fusion
  81.4 4.3 %collective-permute-start.3 = (f32[72,128]{1,0:T(8,128)S(1)}, f32[72,128]{1,0:T(8,128)S(1)}, u32[]{:S(2)}, u32[]{:S(2)}) collective-permute-start(f32[72,128]{1,0:T(8,128)S(1)} %get-tuple-element.6), channel_id=1, source_target_pairs={{0,448},{32,480},{64,0},{96,32},{128,64},{160,96},{192,128},{224,1... | collective-permute-start | bytes 110600 | tf_op jit(solution)/shard_map/ppermute | solution.py:269
  85.8 1.3 %collective-permute-done.3 = f32[72,128]{1,0:T(8,128)S(1)} collective-permute-done((f32[72,128]{1,0:T(8,128)S(1)}, f32[72,128]{1,0:T(8,128)S(1)}, u32[]{:S(2)}, u32[]{:S(2)}) %collective-permute-start.3) | collective-permute-done | bytes 36896 | tf_op jit(solution)/shard_map/ppermute | solution.py:269
  87.1 0.7 broadcast_in_dim.52
  87.7 6.9 %all-to-all-start.2 = ((bf16[8,72,128]{2,1,0:T(8,128)(2,1)}), bf16[8,72,128]{2,1,0:T(8,128)(2,1)S(1)}, u32[]{:S(2)}, u32[]{:S(2)}) async-start(bf16[8,72,128]{2,1,0:T(8,128)(2,1)} %broadcast_in_dim.52), calls=%async_computation.2 | async-start | bytes 294912 | tf_op jit(solution)/shard_map/all_to_all | solution.py:271
  94.6 1.6 %copy-done.2 = bf16[1024,1024]{1,0:T(8,128)(2,1)S(1)} copy-done((bf16[1024,1024]{1,0:T(8,128)(2,1)S(1)}, bf16[1024,1024]{1,0:T(8,128)(2,1)}, u32[]{:S(2)}) %copy-start.2) | copy-done | bytes 2097176
  96.2 5.2 %shard_map.79 = bf16[8,576,128]{2,1,0:T(8,128)(2,1)} custom-call(s32[19]{0:T(128)S(1)} %pad_add_fusion.meta, bf16[8,576,128]{2,1,0:T(8,128)(2,1)S(1)} %bitcast.24, bf16[8,576,128]{2,1,0:T(8,128)(2,1)} %collective-permute-done.1.kt_ref.other_ref, bf16[1024,1024]{1,0:T(8,128)(2,1)S(1)} %copy-done.2), custom_call_target="tpu_custom_call" | custom-call | flops 1207959552 | bytes 8388608 | tf_op jit(solution)/shard_map/pallas_call | solution.py:159
  101.4 0.0 all-to-all-done.2
  101.4 0.7 copy.9
  (6 shorter events, 0.0 us)
Async XLA Ops:
  1.4 13.7 %collective-permute-start = (bf16[144,128]{1,0:T(8,128)(2,1)S(1)}, bf16[144,128]{1,0:T(8,128)(2,1)S(1)}, u32[]{:S(2)}, u32[]{:S(2)}) collective-permute-start(bf16[144,128]{1,0:T(8,128)(2,1)S(1)} %fusion), channel_id=1, source_target_pairs={{0,64},{32,96},{64,128},{96,160},{128,192},{160,224},{192,256},{22... | collective-permute-start | bytes 110600 | tf_op jit(solution)/shard_map/ppermute | solution.py:186
  15.4 29.4 %copy-start.5 = (s32[16]{0:T(128)S(1)}, s32[16]{0:T(128)}, u32[]{:S(2)}) copy-start(s32[16]{0:T(128)} %param.11) | copy-start | bytes 196
  15.5 29.5 %copy-start = (bf16[128,8,576]{0,2,1:T(8,128)(2,1)S(1)}, bf16[128,8,576]{0,2,1:T(8,128)(2,1)}, u32[]{:S(2)}) copy-start(bf16[128,8,576]{0,2,1:T(8,128)(2,1)} %param.6) | copy-start | bytes 3538948
  15.5 29.5 %copy-start.3 = (bf16[128,8,576]{0,2,1:T(8,128)(2,1)S(1)}, bf16[128,8,576]{0,2,1:T(8,128)(2,1)}, u32[]{:S(2)}) copy-start(bf16[128,8,576]{0,2,1:T(8,128)(2,1)} %param.7) | copy-start | bytes 3538948
  15.5 29.5 %copy-start.4 = (f32[128,8]{0,1:T(8,128)S(1)}, f32[128,8]{0,1:T(8,128)}, u32[]{:S(2)}) copy-start(f32[128,8]{0,1:T(8,128)} %param.10) | copy-start | bytes 12292
  39.9 10.7 %collective-permute-start.1 = (bf16[8,576,128]{2,1,0:T(8,128)(2,1)S(1)}, bf16[8,576,128]{2,1,0:T(8,128)(2,1)}, u32[]{:S(2)}, u32[]{:S(2)}) collective-permute-start(bf16[8,576,128]{2,1,0:T(8,128)(2,1)S(1)} %bitcast.22), channel_id=1, source_target_pairs={{0,1},{1,0},{2,3},{3,2},{4,5},{5,4},{6,7},{7,6},{8,9},{9,8},{10,11... | collective-permute-start | bytes 3538952 | tf_op jit(solution)/shard_map/ppermute | solution.py:192
  59.3 3.9 %collective-permute-start.2 = (bf16[8,288,128]{2,1,0:T(8,128)(2,1)S(1)}, bf16[8,288,128]{2,1,0:T(8,128)(2,1)S(1)}, u32[]{:S(2)}, u32[]{:S(2)}) collective-permute-start(bf16[8,288,128]{2,1,0:T(8,128)(2,1)S(1)} %get-tuple-element.5), channel_id=1, source_target_pairs={{0,1},{1,0},{2,3},{3,2},{4,5},{5,4},{6,7},{7,6},{8,9},{9,8},{10,11... | collective-permute-start | bytes 1769480 | tf_op jit(solution)/shard_map/ppermute | solution.py:235
  63.2 1.6 %copy-start.1 = (bf16[1024,1024]{1,0:T(8,128)(2,1)S(1)}, bf16[1024,1024]{1,0:T(8,128)(2,1)}, u32[]{:S(2)}) copy-start(bf16[1024,1024]{1,0:T(8,128)(2,1)} %get-tuple-element.4.g_ref) | copy-start | bytes 6291460
  81.4 5.6 %collective-permute-start.3 = (f32[72,128]{1,0:T(8,128)S(1)}, f32[72,128]{1,0:T(8,128)S(1)}, u32[]{:S(2)}, u32[]{:S(2)}) collective-permute-start(f32[72,128]{1,0:T(8,128)S(1)} %get-tuple-element.6), channel_id=1, source_target_pairs={{0,448},{32,480},{64,0},{96,32},{128,64},{160,96},{192,128},{224,1... | collective-permute-start | bytes 110600 | tf_op jit(solution)/shard_map/ppermute | solution.py:269
  87.7 13.6 %all-to-all-start.2 = ((bf16[8,72,128]{2,1,0:T(8,128)(2,1)}), bf16[8,72,128]{2,1,0:T(8,128)(2,1)S(1)}, u32[]{:S(2)}, u32[]{:S(2)}) async-start(bf16[8,72,128]{2,1,0:T(8,128)(2,1)} %broadcast_in_dim.52), calls=%async_computation.2 | async-start | bytes 294912 | tf_op jit(solution)/shard_map/all_to_all | solution.py:271
  94.6 1.6 %copy-start.2 = (bf16[1024,1024]{1,0:T(8,128)(2,1)S(1)}, bf16[1024,1024]{1,0:T(8,128)(2,1)}, u32[]{:S(2)}) copy-start(bf16[1024,1024]{1,0:T(8,128)(2,1)} %get-tuple-element.4.g_ref) | copy-start | bytes 6291460

commit v2 on v1

v2 whole, which is shorter than its diff:
```python
import math

import jax
import jax.numpy as jnp
from jax import lax
from jax.experimental import pallas as pl
from jax.experimental.pallas import tpu as pltpu
from jax.sharding import Mesh
from jax.sharding import PartitionSpec as P

SEQ_GROUP = 8
TOK = 128
WIN = SEQ_GROUP * TOK
KDIM = 576
HALF = KDIM // 2
PIECE = KDIM // 4
HEADS = 8
PAIRS = HEADS // 2
BLOCKS = [slice(j * TOK, (j + 1) * TOK) for j in range(SEQ_GROUP)]
SCALE = 192.0 ** (-0.5)
SCALE_LOG2 = SCALE * math.log2(math.e)
HIDDEN = -1e30


def key_rows(kt_ref, k_ref):
    for j in range(SEQ_GROUP):
        k_ref[j * TOK : (j + 1) * TOK, :] = kt_ref[j].T


def hidden_bias(meta, bias_ref):
    me, seq = meta[1], meta[2]
    query_pos = seq * TOK + lax.broadcasted_iota(jnp.int32, (1, TOK), 1)
    start = jnp.zeros((1, TOK), jnp.int32)
    end = jnp.int32(0)
    for m in range(16):
        end = end + meta[3 + m]
        start = jnp.where(query_pos >= end, end, start)
    row = lax.broadcasted_iota(jnp.int32, (TOK, TOK), 0)
    for j in range(SEQ_GROUP):
        block = seq - me + j - jnp.where(j > me, SEQ_GROUP, 0)
        key_pos = block * TOK + row
        seen = (key_pos >= start) & (key_pos <= query_pos)
        bias_ref[j * TOK : (j + 1) * TOK, :] = jnp.where(seen, 0.0, HIDDEN)


def both(a, b):
    return jnp.concatenate([a, b], axis=1)


def scores(k_ref, bias_ref, queries, s_ref):
    s_ref[...] = jnp.dot(k_ref[...], queries, preferred_element_type=jnp.float32)
    peak = jnp.full((8, 2 * TOK), HIDDEN, jnp.float32)
    for rows in BLOCKS:
        bias = bias_ref[rows, :]
        s = s_ref[rows, :] + both(bias, bias)
        s_ref[rows, :] = s
        peak = jnp.maximum(peak, jnp.max(s.reshape(TOK // 8, 8, 2 * TOK), axis=0))
    return jnp.max(peak, axis=0, keepdims=True)


def exponentials(s_ref, peak):
    total = jnp.zeros((8, 2 * TOK), jnp.float32)
    for rows in BLOCKS:
        e = jnp.exp2((s_ref[rows, :] - peak) * SCALE_LOG2)
        s_ref[rows, :] = e
        total = total + jnp.sum(e.reshape(TOK // 8, 8, 2 * TOK), axis=0)
    return jnp.sum(total, axis=0, keepdims=True)


def pair_queries(student, sq_ref, tq_ref, i):
    return both(
        jnp.where(student, sq_ref[2 * i], tq_ref[2 * i]),
        jnp.where(student, sq_ref[2 * i + 1], tq_ref[2 * i + 1]),
    )


def pair_weight(lw_ref, i, student):
    weight = both(lw_ref[2 * i : 2 * i + 1, :], lw_ref[2 * i + 1 : 2 * i + 2, :])
    return weight * jnp.where(student, SCALE, -SCALE)


def all_pairs(meta, student, kt_ref, sq_ref, tq_ref, lw_ref, k_ref, bias_ref, s_ref, use):
    key_rows(kt_ref, k_ref)
    hidden_bias(meta, bias_ref)
    peak = scores(k_ref, bias_ref, pair_queries(student, sq_ref, tq_ref, 0), s_ref.at[0])
    for i in range(PAIRS):
        later = None
        if i + 1 < PAIRS:
            queries = pair_queries(student, sq_ref, tq_ref, i + 1)
            later = scores(k_ref, bias_ref, queries, s_ref.at[(i + 1) % 2])
        total = exponentials(s_ref.at[i % 2], peak)
        factor = pair_weight(lw_ref, i, student) / total
        for rows in BLOCKS:
            use(i, rows, s_ref[i % 2, rows, :] * factor)
        peak = later


def pair_lanes(i):
    return slice(i * 2 * TOK, (i + 1) * 2 * TOK)


def first_kernel(meta, kt_ref, sq_ref, tq_ref, lw_ref, p_ref, k_ref, bias_ref, s_ref):
    def use(i, rows, probs):
        p_ref[rows, pair_lanes(i)] = probs

    student = meta[0] == 0
    all_pairs(meta, student, kt_ref, sq_ref, tq_ref, lw_ref, k_ref, bias_ref, s_ref, use)


def key_grad_half(sq_ref, half, g):
    rows = pl.ds(pl.multiple_of(half * HALF, HALF), HALF)
    queries = jnp.concatenate([sq_ref[h, rows, :] for h in range(HEADS)], axis=1)
    return lax.dot_general(
        queries, g, (((1,), (1,)), ((), ())), preferred_element_type=jnp.float32
    )


def second_kernel(
    meta, kt_ref, sq_ref, tq_ref, lw_ref, p_ref, g_ref, kg_ref, k_ref, bias_ref, s_ref
):
    student = meta[0] == 1

    def use(i, rows, probs):
        g_ref[rows, pair_lanes(i)] = (p_ref[rows, pair_lanes(i)] + probs).astype(jnp.bfloat16)

    all_pairs(meta, student, kt_ref, sq_ref, tq_ref, lw_ref, k_ref, bias_ref, s_ref, use)
    grad = key_grad_half(sq_ref, 1 - meta[0], g_ref[...]).astype(jnp.bfloat16)
    for j in range(SEQ_GROUP):
        kg_ref[j] = grad[:, j * TOK : (j + 1) * TOK]


def query_kernel(
    meta, mine_ref, other_ref, g_ref, kept_ref, out_ref, kept_out_ref, kt_ref, stage_ref, sems
):
    kept_out_ref[...] = kept_ref[...]

    @pl.when(meta[0] == 0)
    def _():
        for j in range(SEQ_GROUP):
            kt_ref[:, j * TOK : (j + 1) * TOK] = mine_ref[j]

    @pl.when(meta[0] == 1)
    def _():
        for j in range(SEQ_GROUP):
            kt_ref[:, j * TOK : (j + 1) * TOK] = other_ref[j]

    copies = []
    for i in range(PAIRS):
        grad = jnp.dot(
            kt_ref[...], g_ref[:, pair_lanes(i)], preferred_element_type=jnp.float32
        ).astype(jnp.bfloat16)
        stage_ref[2 * i] = grad[:, :TOK]
        stage_ref[2 * i + 1] = grad[:, TOK:]
        pair = pl.ds(2 * i, 2)
        copies.append(pltpu.make_async_copy(stage_ref.at[pair], out_ref.at[pair], sems.at[i]))
        copies[-1].start()
    for copy in copies:
        copy.wait()


def key_kernel(meta, sq_ref, g_ref, got_ref, out_ref):
    grad = key_grad_half(sq_ref, meta[0], g_ref[...])
    for j in range(SEQ_GROUP):
        lanes = slice(j * TOK, (j + 1) * TOK)
        out_ref[j] = (grad[:, lanes] + got_ref[j].astype(jnp.float32)).astype(jnp.bfloat16)


def call(kernel, out_specs, out_shape, scratch, mib, flops, args):
    in_vmem = pl.BlockSpec(memory_space=pltpu.VMEM)
    return pl.pallas_call(
        kernel,
        in_specs=[pl.BlockSpec(memory_space=pltpu.SMEM)] + [in_vmem] * (len(args) - 1),
        out_specs=out_specs,
        out_shape=out_shape,
        scratch_shapes=scratch,
        compiler_params=pltpu.CompilerParams(vmem_limit_bytes=mib << 20),
        cost_estimate=pl.CostEstimate(flops=flops, bytes_accessed=8 << 20, transcendentals=1 << 20),
    )(*args)


def on_device(student_query, teacher_query, student_keys, teacher_keys, loss_weight, doc_lengths):
    core = lax.axis_index("c")
    x = lax.axis_index("x")
    me = lax.axis_index(("zi", "y"))
    seq = lax.axis_index(("zo", "zi", "y"))
    meta = jnp.concatenate([jnp.stack([core, me, seq]).astype(jnp.int32), doc_lengths])
    sq = student_query.transpose(1, 2, 0)
    tq = teacher_query.transpose(1, 2, 0)
    lw = loss_weight.T

    table = jnp.where(core == 0, student_keys.T, teacher_keys.T)
    own = lax.dynamic_slice_in_dim(table, x * PIECE, PIECE, 0)
    before = lax.ppermute(own, ("zo", "zi"), [(i, i + 2) for i in range(14)])
    later = (jnp.arange(SEQ_GROUP) >= me)[:, None, None, None]
    outgoing = jnp.broadcast_to(jnp.where(later, own, before), (SEQ_GROUP, 4, PIECE, TOK))
    mine = lax.all_to_all(
        outgoing.reshape(SEQ_GROUP * 4, PIECE, TOK), ("zi", "y", "x"), 0, 0, tiled=True
    ).reshape(SEQ_GROUP, KDIM, TOK)
    other = lax.ppermute(mine, "c", [(0, 1), (1, 0)])

    in_vmem = pl.BlockSpec(memory_space=pltpu.VMEM)
    scratch = [
        pltpu.VMEM((WIN, KDIM), jnp.bfloat16),
        pltpu.VMEM((WIN, TOK), jnp.float32),
        pltpu.VMEM((2, WIN, 2 * TOK), jnp.float32),
    ]
    matmul = 2 * WIN * HEADS * TOK * KDIM
    probs = call(
        first_kernel,
        in_vmem,
        jax.ShapeDtypeStruct((WIN, HEADS * TOK), jnp.float32),
        scratch,
        12,
        matmul,
        (meta, mine, sq, tq, lw),
    )
    half_grad = jax.ShapeDtypeStruct((SEQ_GROUP, HALF, TOK), jnp.bfloat16)
    score_grad, sent = call(
        second_kernel,
        [in_vmem, in_vmem],
        [jax.ShapeDtypeStruct((WIN, HEADS * TOK), jnp.bfloat16), half_grad],
        scratch,
        12,
        matmul * 3 // 2,
        (meta, other, sq, tq, lw, probs),
    )
    got = lax.ppermute(sent, "c", [(0, 1), (1, 0)])
    partial = call(key_kernel, in_vmem, half_grad, [], 6, matmul // 2, (meta, sq, score_grad, got))
    rows = HALF // 4
    terms = lax.all_to_all(
        partial.reshape(SEQ_GROUP * 4, rows, TOK), ("zi", "y", "x"), 0, 0, tiled=True
    ).reshape(SEQ_GROUP, 4, rows, TOK)
    terms = jnp.sum(terms.astype(jnp.float32), axis=1)
    here = (jnp.arange(SEQ_GROUP) >= me)[:, None, None]
    kept = jnp.sum(jnp.where(here, terms, 0.0), axis=0)
    returned = jnp.sum(jnp.where(here, 0.0, terms), axis=0)
    returned = lax.ppermute(returned, ("zo", "zi"), [(i + 2, i) for i in range(14)])
    query_grad, kept = call(
        query_kernel,
        [pl.BlockSpec(memory_space=pl.ANY), in_vmem],
        [
            jax.ShapeDtypeStruct((HEADS, KDIM, TOK), jnp.bfloat16),
            jax.ShapeDtypeStruct((rows, TOK), jnp.float32),
        ],
        [
            pltpu.VMEM((KDIM, WIN), jnp.bfloat16),
            pltpu.VMEM((HEADS, KDIM, TOK), jnp.bfloat16),
            pltpu.SemaphoreType.DMA((PAIRS,)),
        ],
        8,
        matmul,
        (meta, mine, other, score_grad, kept),
    )
    share = (kept + returned).astype(jnp.bfloat16)
    key_grad = lax.all_to_all(
        jnp.broadcast_to(share, (8, rows, TOK)), ("c", "x"), 0, 0, tiled=True
    ).reshape(KDIM, TOK)
    return (query_grad.transpose(2, 0, 1), key_grad.T)


def solution(mesh):
    fine = Mesh(mesh.devices.reshape(8, 2, 4, 4, 2), ("zo", "zi", "y", "x", "c"))
    seq, head = ("zo", "zi", "y"), ("x", "c")
    return jax.shard_map(
        on_device,
        mesh=fine,
        in_specs=(
            P(seq, head, None),
            P(seq, head, None),
            P(seq, None),
            P(seq, None),
            P(seq, head),
            P(),
        ),
        out_specs=(P(seq, head, None), P(seq, None)),
        check_vma=False,
    )
```

time: 103 us -> 87.6 us (0.85)
  blocking collectives: 38.9 us -> 50.8 us
  starting transfers between devices: 23.8 us -> 13.8 us
  Pallas kernels: 21.5 us -> 14.3 us
  waiting for transfers between devices: 11.2 us -> 5.23 us
  local copies, waits for them, and re-layouts: 4.7 us -> 0.86 us
    all_to_all x0 -> x1, blocking collectives: none -> 11 us  [on_device(): lax.all_to_all(jnp.broadcast_to(share, (8, rows, TOK)), ('c', 'x'), 0, 0,...]
    pallas_call x4, Pallas kernels: 21.5 us -> 14.3 us  [call(): pl.pallas_call(kernel, in_specs=[pl.BlockSpec(memory_space=pltpu.SMEM)] +...]
    all_to_all x1 -> x0, starting transfers between devices: 6.85 us -> none  [on_device(): lax.all_to_all(jnp.broadcast_to(share, (8, rows, TOK)), ('c', 'x'), 0, 0,...]
    ppermute x2, waiting for transfers between devices: 9.24 us -> 3.26 us  [the longest x1 2.23 us: on_device(): lax.ppermute(returned, ('zo', 'zi'), [(i + 2, i) for i in range(14)])]
    unnamed x13 -> x9, local copies, waits for them, and re-layouts: 3.87 us -> 0.69 us
    ppermute x2, starting transfers between devices: 10.1 us -> 7.02 us  [the longest x1 5.73 us: on_device(): before = lax.ppermute(own, ('zo', 'zi'), [(i, i + 2) for i in range(14)])]
  transfers between devices with their start and end apart: 5 -> 4, of which waited for: 3 -> 3; matrix products, arithmetic and copies ran while one was open for 0% -> 0% of each run, Pallas kernels for 11% -> 8%
where the time goes in v2:
time: 87.6 us; the launch traced here: 87 us
  blocking collectives  50.8 us (58%)
  Pallas kernels  14.3 us (16%)
  starting transfers between devices  13.8 us (16%)
  waiting for transfers between devices  5.23 us (6%)
  other arithmetic  1.17 us (1%)
    all_to_all x1, blocking collectives, on_device(): lax.all_to_all(outgoing.reshape(SEQ_GROUP * 4, PIECE, TOK), ('zi', 'y', '...  25.4 us
    all_to_all x1, blocking collectives, on_device(): lax.all_to_all(partial.reshape(SEQ_GROUP * 4, rows, TOK), ('zi', 'y', 'x'...  14.4 us
    pallas_call x4, Pallas kernels, call(): pl.pallas_call(kernel, in_specs=[pl.BlockSpec(memory_space=pltpu.SMEM)] +...  14.3 us
    all_to_all x1, blocking collectives, on_device(): lax.all_to_all(jnp.broadcast_to(share, (8, rows, TOK)), ('c', 'x'), 0, 0,...  11 us
    ppermute x1, starting transfers between devices, on_device(): before = lax.ppermute(own, ('zo', 'zi'), [(i, i + 2) for i in range(14)])  5.73 us
    ppermute x1, starting transfers between devices, on_device(): other = lax.ppermute(mine, 'c', [(0, 1), (1, 0)])  4.9 us
    ppermute x1, waiting for transfers between devices, on_device(): lax.ppermute(returned, ('zo', 'zi'), [(i + 2, i) for i in range(14)])  2.23 us
    ppermute x1, waiting for transfers between devices, on_device(): got = lax.ppermute(sent, 'c', [(0, 1), (1, 0)])  1.97 us
  transfers between devices with their start and end apart: 4, of which 3 were waited for; matrix products, arithmetic and copies ran while one was open for 0% of the time, Pallas kernels for 8%

profile of v2, /device:TPU:1, one launch (start us, length us, event | category | flops | bytes accessed | tf_op | source)
XLA Modules:
  0.0 87.0 jit_solution(1174795741111525669)
XLA Ops:
  0.6 0.8 fusion
  1.4 5.7 %collective-permute-start = (bf16[144,128]{1,0:T(8,128)(2,1)S(1)}, bf16[144,128]{1,0:T(8,128)(2,1)S(1)}, u32[]{:S(2)}, u32[]{:S(2)}) collective-permute-start(bf16[144,128]{1,0:T(8,128)(2,1)S(1)} %fusion), channel_id=1, source_target_pairs={{0,64},{32,96},{64,128},{96,160},{128,192},{160,224},{192,256},{22... | collective-permute-start | bytes 110600 | tf_op jit(solution)/shard_map/ppermute | solution.py:193
  7.2 1.0 %collective-permute-done = bf16[144,128]{1,0:T(8,128)(2,1)S(1)} collective-permute-done((bf16[144,128]{1,0:T(8,128)(2,1)S(1)}, bf16[144,128]{1,0:T(8,128)(2,1)S(1)}, u32[]{:S(2)}, u32[]{:S(2)}) %collective-permute-start) | collective-permute-done | bytes 36896 | tf_op jit(solution)/shard_map/ppermute | solution.py:193
  8.2 0.1 broadcast_select_fusion
  8.3 0.2 broadcast_in_dim.49
  8.5 0.0 copy-start.3
  8.5 0.0 copy-start
  8.5 0.0 copy-start.1
  8.5 0.0 copy-start.2
  8.5 25.4 %all_to_all.15 = bf16[32,144,128]{2,1,0:T(8,128)(2,1)S(1)} all-to-all(bf16[32,144,128]{2,1,0:T(8,128)(2,1)S(1)} %bitcast.29), channel_id=1, replica_groups=mesh['zo'=8,'zi'=2,'y'=4,'x'=4,'c'=2] {'zi','y','x'}, dimensions={0} | all-to-all | bytes 2359296 | tf_op jit(solution)/shard_map/all_to_all | solution.py:196
  33.9 4.9 %collective-permute-start.1 = (bf16[8,576,128]{2,1,0:T(8,128)(2,1)S(1)}, bf16[8,576,128]{2,1,0:T(8,128)(2,1)}, u32[]{:S(2)}, u32[]{:S(2)}) collective-permute-start(bf16[8,576,128]{2,1,0:T(8,128)(2,1)S(1)} %bitcast.21), channel_id=1, source_target_pairs={{0,1},{1,0},{2,3},{3,2},{4,5},{5,4},{6,7},{7,6},{8,9},{9,8},{10,11... | collective-permute-start | bytes 3538952 | tf_op jit(solution)/shard_map/ppermute | solution.py:199
  38.8 0.0 copy-done.3
  38.8 0.1 pad_add_fusion.meta
  38.9 0.0 copy-done
  38.9 0.0 copy-done.1
  38.9 0.0 copy-done.2
  38.9 3.4 %shard_map.77.p_ref = f32[1024,1024]{1,0:T(8,128)S(1)} custom-call(s32[19]{0:T(128)S(1)} %pad_add_fusion.meta, bf16[8,576,128]{2,1,0:T(8,128)(2,1)S(1)} %bitcast.22, bf16[8,576,128]{2,1,0:T(8,128)(2,1)S(1)} %bitcast.18, bf16[8,576,128]{2,1,0:T(8,128)(2,1)S(1)} %bitcast.24, f32[8,128]{1,0:T(8,128)S(1)} %bitcast.27), custom_call_target="tpu_custom_call" | custom-call | flops 1207959552 | bytes 8388608 | tf_op jit(solution)/shard_map/pallas_call | solution.py:170
  42.4 0.0 collective-permute-done.1.kt_ref.other_ref
  42.4 5.6 %shard_map.78 = (bf16[1024,1024]{1,0:T(8,128)(2,1)S(1)}, bf16[8,288,128]{2,1,0:T(8,128)(2,1)S(1)}) custom-call(s32[19]{0:T(128)S(1)} %pad_add_fusion.meta, bf16[8,576,128]{2,1,0:T(8,128)(2,1)} %collective-permute-done.1.kt_ref.other_ref, bf16[8,576,128]{2,1,0:T(8,128)(2,1)S(1)} %bitcast.19, bf16[8,576,128]{2,1,0:T(8,128)(2,1)S(1)} %bitcast.25, ...), custom_call_target="tpu_custom_call" | custom-call | flops 1811939328 | bytes 8388608 | tf_op jit(solution)/shard_map/pallas_call | solution.py:170
  48.0 1.9 %collective-permute-start.2 = (bf16[8,288,128]{2,1,0:T(8,128)(2,1)S(1)}, bf16[8,288,128]{2,1,0:T(8,128)(2,1)S(1)}, u32[]{:S(2)}, u32[]{:S(2)}) collective-permute-start(bf16[8,288,128]{2,1,0:T(8,128)(2,1)S(1)} %get-tuple-element.7), channel_id=1, source_target_pairs={{0,1},{1,0},{2,3},{3,2},{4,5},{5,4},{6,7},{7,6},{8,9},{9,8},{10,11... | collective-permute-start | bytes 1769480 | tf_op jit(solution)/shard_map/ppermute | solution.py:227
  49.9 2.0 %collective-permute-done.2.got_ref = bf16[8,288,128]{2,1,0:T(8,128)(2,1)S(1)} collective-permute-done((bf16[8,288,128]{2,1,0:T(8,128)(2,1)S(1)}, bf16[8,288,128]{2,1,0:T(8,128)(2,1)S(1)}, u32[]{:S(2)}, u32[]{:S(2)}) %collective-permute-start.2) | collective-permute-done | bytes 589856 | tf_op jit(solution)/shard_map/ppermute | solution.py:227
  51.9 1.4 %shard_map.79 = bf16[8,288,128]{2,1,0:T(8,128)(2,1)S(1)} custom-call(s32[19]{0:T(128)S(1)} %pad_add_fusion.meta, bf16[8,576,128]{2,1,0:T(8,128)(2,1)S(1)} %bitcast.20, bf16[1024,1024]{1,0:T(8,128)(2,1)S(1)} %get-tuple-element.6.g_ref, bf16[8,288,128]{2,1,0:T(8,128)(2,1)S(1)} %collective-permute-done.2.got_ref), custom_call_target="tpu_custom_call" | custom-call | flops 603979776 | bytes 8388608 | tf_op jit(solution)/shard_map/pallas_call | solution.py:170
  53.2 14.4 %all_to_all.16 = bf16[32,72,128]{2,1,0:T(8,128)(2,1)S(1)} all-to-all(bf16[32,72,128]{2,1,0:T(8,128)(2,1)S(1)} %bitcast.26), channel_id=1, replica_groups=mesh['zo'=8,'zi'=2,'y'=4,'x'=4,'c'=2] {'zi','y','x'}, dimensions={0} | all-to-all | bytes 1179648 | tf_op jit(solution)/shard_map/all_to_all | solution.py:230
  67.7 0.1 convert_reduce_fusion
  67.7 0.1 select_reduce_fusion
  67.8 1.3 %collective-permute-start.3 = (f32[72,128]{1,0:T(8,128)S(1)}, f32[72,128]{1,0:T(8,128)S(1)}, u32[]{:S(2)}, u32[]{:S(2)}) collective-permute-start(f32[72,128]{1,0:T(8,128)S(1)} %get-tuple-element.10), channel_id=1, source_target_pairs={{64,0},{96,32},{128,64},{160,96},{192,128},{224,160},{256,192},{28... | collective-permute-start | bytes 110600 | tf_op jit(solution)/shard_map/ppermute | solution.py:237
  69.2 3.9 %shard_map.80 = (bf16[8,576,128]{2,1,0:T(8,128)(2,1)}, f32[72,128]{1,0:T(8,128)S(1)}) custom-call(s32[19]{0:T(128)S(1)} %pad_add_fusion.meta, bf16[8,576,128]{2,1,0:T(8,128)(2,1)S(1)} %bitcast.23, bf16[8,576,128]{2,1,0:T(8,128)(2,1)} %collective-permute-done.1.kt_ref.other_ref, bf16[1024,1024]{1,0:T(8,128)(2,1)S(1)} %get-tuple-element.6.g_ref, ...), custom_call_target="tpu_custom_call" | custom-call | flops 1207959552 | bytes 8388608 | tf_op jit(solution)/shard_map/pallas_call | solution.py:170
  73.1 2.2 %collective-permute-done.3 = f32[72,128]{1,0:T(8,128)S(1)} collective-permute-done((f32[72,128]{1,0:T(8,128)S(1)}, f32[72,128]{1,0:T(8,128)S(1)}, u32[]{:S(2)}, u32[]{:S(2)}) %collective-permute-start.3) | collective-permute-done | bytes 36896 | tf_op jit(solution)/shard_map/ppermute | solution.py:237
  75.3 11.0 %all_to_all.17 = bf16[8,72,128]{2,1,0:T(8,128)(2,1)S(1)} all-to-all(bf16[8,72,128]{2,1,0:T(8,128)(2,1)S(1)} %broadcast_in_dim.52), channel_id=1, replica_groups=mesh['zo'=8,'zi'=2,'y'=4,'x'=4,'c'=2] {'c','x'}, dimensions={0} | all-to-all | bytes 294912 | tf_op jit(solution)/shard_map/all_to_all | solution.py:255
  86.4 0.7 copy.9
  (3 shorter events, 0.0 us)
Async XLA Ops:
  1.4 6.8 %collective-permute-start = (bf16[144,128]{1,0:T(8,128)(2,1)S(1)}, bf16[144,128]{1,0:T(8,128)(2,1)S(1)}, u32[]{:S(2)}, u32[]{:S(2)}) collective-permute-start(bf16[144,128]{1,0:T(8,128)(2,1)S(1)} %fusion), channel_id=1, source_target_pairs={{0,64},{32,96},{64,128},{96,160},{128,192},{160,224},{192,256},{22... | collective-permute-start | bytes 110600 | tf_op jit(solution)/shard_map/ppermute | solution.py:193
  8.5 30.3 %copy-start.3 = (s32[16]{0:T(128)S(1)}, s32[16]{0:T(128)}, u32[]{:S(2)}) copy-start(s32[16]{0:T(128)} %param.11) | copy-start | bytes 196
  8.5 30.4 %copy-start = (bf16[128,8,576]{0,2,1:T(8,128)(2,1)S(1)}, bf16[128,8,576]{0,2,1:T(8,128)(2,1)}, u32[]{:S(2)}) copy-start(bf16[128,8,576]{0,2,1:T(8,128)(2,1)} %param.6) | copy-start | bytes 3538948
  8.5 30.4 %copy-start.1 = (bf16[128,8,576]{0,2,1:T(8,128)(2,1)S(1)}, bf16[128,8,576]{0,2,1:T(8,128)(2,1)}, u32[]{:S(2)}) copy-start(bf16[128,8,576]{0,2,1:T(8,128)(2,1)} %param.7) | copy-start | bytes 3538948
  8.5 30.4 %copy-start.2 = (f32[128,8]{0,1:T(8,128)S(1)}, f32[128,8]{0,1:T(8,128)}, u32[]{:S(2)}) copy-start(f32[128,8]{0,1:T(8,128)} %param.10) | copy-start | bytes 12292
  33.9 8.5 %collective-permute-start.1 = (bf16[8,576,128]{2,1,0:T(8,128)(2,1)S(1)}, bf16[8,576,128]{2,1,0:T(8,128)(2,1)}, u32[]{:S(2)}, u32[]{:S(2)}) collective-permute-start(bf16[8,576,128]{2,1,0:T(8,128)(2,1)S(1)} %bitcast.21), channel_id=1, source_target_pairs={{0,1},{1,0},{2,3},{3,2},{4,5},{5,4},{6,7},{7,6},{8,9},{9,8},{10,11... | collective-permute-start | bytes 3538952 | tf_op jit(solution)/shard_map/ppermute | solution.py:199
  48.0 3.9 %collective-permute-start.2 = (bf16[8,288,128]{2,1,0:T(8,128)(2,1)S(1)}, bf16[8,288,128]{2,1,0:T(8,128)(2,1)S(1)}, u32[]{:S(2)}, u32[]{:S(2)}) collective-permute-start(bf16[8,288,128]{2,1,0:T(8,128)(2,1)S(1)} %get-tuple-element.7), channel_id=1, source_target_pairs={{0,1},{1,0},{2,3},{3,2},{4,5},{5,4},{6,7},{7,6},{8,9},{9,8},{10,11... | collective-permute-start | bytes 1769480 | tf_op jit(solution)/shard_map/ppermute | solution.py:227
  67.8 7.5 %collective-permute-start.3 = (f32[72,128]{1,0:T(8,128)S(1)}, f32[72,128]{1,0:T(8,128)S(1)}, u32[]{:S(2)}, u32[]{:S(2)}) collective-permute-start(f32[72,128]{1,0:T(8,128)S(1)} %get-tuple-element.10), channel_id=1, source_target_pairs={{64,0},{96,32},{128,64},{160,96},{192,128},{224,160},{256,192},{28... | collective-permute-start | bytes 110600 | tf_op jit(solution)/shard_map/ppermute | solution.py:237

commit v3 on v2

--- a/solution.py
+++ b/solution.py
@@ -48,11 +48,11 @@
 
 
 def scores(k_ref, bias_ref, queries, s_ref):
-    s_ref[...] = jnp.dot(k_ref[...], queries, preferred_element_type=jnp.float32)
     peak = jnp.full((8, 2 * TOK), HIDDEN, jnp.float32)
     for rows in BLOCKS:
         bias = bias_ref[rows, :]
-        s = s_ref[rows, :] + both(bias, bias)
+        s = jnp.dot(k_ref[rows, :], queries, preferred_element_type=jnp.float32)
+        s = s + both(bias, bias)
         s_ref[rows, :] = s
         peak = jnp.maximum(peak, jnp.max(s.reshape(TOK // 8, 8, 2 * TOK), axis=0))
     return jnp.max(peak, axis=0, keepdims=True)
@@ -158,11 +158,10 @@
         copy.wait()
 
 
-def key_kernel(meta, sq_ref, g_ref, got_ref, out_ref):
+def own_key_kernel(meta, sq_ref, g_ref, out_ref):
     grad = key_grad_half(sq_ref, meta[0], g_ref[...])
-    for j in range(SEQ_GROUP):
-        lanes = slice(j * TOK, (j + 1) * TOK)
-        out_ref[j] = (grad[:, lanes] + got_ref[j].astype(jnp.float32)).astype(jnp.bfloat16)
+    for j, lanes in enumerate(BLOCKS):
+        out_ref[j] = grad[:, lanes]
 
 
 def call(kernel, out_specs, out_shape, scratch, mib, flops, args):
@@ -225,7 +224,16 @@
         (meta, other, sq, tq, lw, probs),
     )
     got = lax.ppermute(sent, "c", [(0, 1), (1, 0)])
-    partial = call(key_kernel, in_vmem, half_grad, [], 6, matmul // 2, (meta, sq, score_grad, got))
+    own_half = call(
+        own_key_kernel,
+        in_vmem,
+        jax.ShapeDtypeStruct((SEQ_GROUP, HALF, TOK), jnp.float32),
+        [],
+        6,
+        matmul // 2,
+        (meta, sq, score_grad),
+    )
+    partial = (own_half + got.astype(jnp.float32)).astype(jnp.bfloat16)
     rows = HALF // 4
     terms = lax.all_to_all(
         partial.reshape(SEQ_GROUP * 4, rows, TOK), ("zi", "y", "x"), 0, 0, tiled=True

time: 87.6 us -> 85.8 us (0.979)
  waiting for transfers between devices: 5.23 us -> 3.87 us
    ppermute x1, waiting for transfers between devices: 1.97 us -> 0.62 us  [on_device(): got = lax.ppermute(sent, 'c', [(0, 1), (1, 0)])]
  transfers between devices with their start and end apart: 4 -> 4, of which waited for: 3 -> 3; matrix products, arithmetic and copies ran while one was open for 0% -> 0% of each run, Pallas kernels for 8% -> 10%
where the time goes in v3:
time: 85.8 us; the launch traced here: 85.2 us
  blocking collectives  50.8 us (59%)
  starting transfers between devices  13.8 us (16%)
  Pallas kernels  13.7 us (16%)
  waiting for transfers between devices  3.87 us (5%)
  other arithmetic  1.33 us (2%)
  local copies, waits for them, and re-layouts  0.86 us (1%)
    all_to_all x1, blocking collectives, on_device(): lax.all_to_all(outgoing.reshape(SEQ_GROUP * 4, PIECE, TOK), ('zi', 'y', '...  25.4 us
    all_to_all x1, blocking collectives, on_device(): lax.all_to_all(partial.reshape(SEQ_GROUP * 4, rows, TOK), ('zi', 'y', 'x'...  14.4 us
    pallas_call x4, Pallas kernels, call(): pl.pallas_call(kernel, in_specs=[pl.BlockSpec(memory_space=pltpu.SMEM)] +...  13.7 us
    all_to_all x1, blocking collectives, on_device(): lax.all_to_all(jnp.broadcast_to(share, (8, rows, TOK)), ('c', 'x'), 0, 0,...  11 us
    ppermute x1, starting transfers between devices, on_device(): before = lax.ppermute(own, ('zo', 'zi'), [(i, i + 2) for i in range(14)])  5.73 us
    ppermute x1, starting transfers between devices, on_device(): other = lax.ppermute(mine, 'c', [(0, 1), (1, 0)])  4.9 us
    ppermute x1, waiting for transfers between devices, on_device(): lax.ppermute(returned, ('zo', 'zi'), [(i + 2, i) for i in range(14)])  2.23 us
    ppermute x1, starting transfers between devices, on_device(): got = lax.ppermute(sent, 'c', [(0, 1), (1, 0)])  1.92 us
  transfers between devices with their start and end apart: 4, of which 3 were waited for; matrix products, arithmetic and copies ran while one was open for 0% of the time, Pallas kernels for 10%

profile of v3, /device:TPU:1, one launch (start us, length us, event | category | flops | bytes accessed | tf_op | source)
XLA Modules:
  0.0 85.2 jit_solution(16579915684789055896)
XLA Ops:
  0.6 0.8 fusion
  1.4 5.7 %collective-permute-start = (bf16[144,128]{1,0:T(8,128)(2,1)S(1)}, bf16[144,128]{1,0:T(8,128)(2,1)S(1)}, u32[]{:S(2)}, u32[]{:S(2)}) collective-permute-start(bf16[144,128]{1,0:T(8,128)(2,1)S(1)} %fusion), channel_id=1, source_target_pairs={{0,64},{32,96},{64,128},{96,160},{128,192},{160,224},{192,256},{22... | collective-permute-start | bytes 110600 | tf_op jit(solution)/shard_map/ppermute | solution.py:192
  7.2 1.0 %collective-permute-done = bf16[144,128]{1,0:T(8,128)(2,1)S(1)} collective-permute-done((bf16[144,128]{1,0:T(8,128)(2,1)S(1)}, bf16[144,128]{1,0:T(8,128)(2,1)S(1)}, u32[]{:S(2)}, u32[]{:S(2)}) %collective-permute-start) | collective-permute-done | bytes 36896 | tf_op jit(solution)/shard_map/ppermute | solution.py:192
  8.2 0.1 broadcast_select_fusion
  8.3 0.2 broadcast_in_dim.49
  8.5 0.0 copy-start.3
  8.5 0.0 copy-start
  8.5 0.0 copy-start.1
  8.5 0.0 copy-start.2
  8.5 25.4 %all_to_all.15 = bf16[32,144,128]{2,1,0:T(8,128)(2,1)S(1)} all-to-all(bf16[32,144,128]{2,1,0:T(8,128)(2,1)S(1)} %bitcast.28), channel_id=1, replica_groups=mesh['zo'=8,'zi'=2,'y'=4,'x'=4,'c'=2] {'zi','y','x'}, dimensions={0} | all-to-all | bytes 2359296 | tf_op jit(solution)/shard_map/all_to_all | solution.py:195
  33.9 4.9 %collective-permute-start.1 = (bf16[8,576,128]{2,1,0:T(8,128)(2,1)S(1)}, bf16[8,576,128]{2,1,0:T(8,128)(2,1)}, u32[]{:S(2)}, u32[]{:S(2)}) collective-permute-start(bf16[8,576,128]{2,1,0:T(8,128)(2,1)S(1)} %bitcast.21), channel_id=1, source_target_pairs={{0,1},{1,0},{2,3},{3,2},{4,5},{5,4},{6,7},{7,6},{8,9},{9,8},{10,11... | collective-permute-start | bytes 3538952 | tf_op jit(solution)/shard_map/ppermute | solution.py:198
  38.8 0.0 copy-done.3
  38.8 0.1 pad_add_fusion.meta
  38.9 0.0 copy-done
  38.9 0.0 copy-done.1
  38.9 0.0 copy-done.2
  38.9 3.2 %shard_map.77.p_ref = f32[1024,1024]{1,0:T(8,128)S(1)} custom-call(s32[19]{0:T(128)S(1)} %pad_add_fusion.meta, bf16[8,576,128]{2,1,0:T(8,128)(2,1)S(1)} %bitcast.22, bf16[8,576,128]{2,1,0:T(8,128)(2,1)S(1)} %bitcast.18, bf16[8,576,128]{2,1,0:T(8,128)(2,1)S(1)} %bitcast.24, f32[8,128]{1,0:T(8,128)S(1)} %bitcast.26), custom_call_target="tpu_custom_call" | custom-call | flops 1207959552 | bytes 8388608 | tf_op jit(solution)/shard_map/pallas_call | solution.py:169
  42.2 0.0 collective-permute-done.1.kt_ref.other_ref
  42.2 5.2 %shard_map.78 = (bf16[1024,1024]{1,0:T(8,128)(2,1)S(1)}, bf16[8,288,128]{2,1,0:T(8,128)(2,1)S(1)}) custom-call(s32[19]{0:T(128)S(1)} %pad_add_fusion.meta, bf16[8,576,128]{2,1,0:T(8,128)(2,1)} %collective-permute-done.1.kt_ref.other_ref, bf16[8,576,128]{2,1,0:T(8,128)(2,1)S(1)} %bitcast.19, bf16[8,576,128]{2,1,0:T(8,128)(2,1)S(1)} %bitcast.25, ...), custom_call_target="tpu_custom_call" | custom-call | flops 1811939328 | bytes 8388608 | tf_op jit(solution)/shard_map/pallas_call | solution.py:169
  47.4 1.9 %collective-permute-start.2 = (bf16[8,288,128]{2,1,0:T(8,128)(2,1)S(1)}, bf16[8,288,128]{2,1,0:T(8,128)(2,1)S(1)}, u32[]{:S(2)}, u32[]{:S(2)}) collective-permute-start(bf16[8,288,128]{2,1,0:T(8,128)(2,1)S(1)} %get-tuple-element.7), channel_id=1, source_target_pairs={{0,1},{1,0},{2,3},{3,2},{4,5},{5,4},{6,7},{7,6},{8,9},{9,8},{10,11... | collective-permute-start | bytes 1769480 | tf_op jit(solution)/shard_map/ppermute | solution.py:226
  49.3 1.3 %shard_map.79 = f32[8,288,128]{2,1,0:T(8,128)S(1)} custom-call(s32[19]{0:T(128)S(1)} %pad_add_fusion.meta, bf16[8,576,128]{2,1,0:T(8,128)(2,1)S(1)} %bitcast.20, bf16[1024,1024]{1,0:T(8,128)(2,1)S(1)} %get-tuple-element.6.g_ref), custom_call_target="tpu_custom_call" | custom-call | flops 603979776 | bytes 8388608 | tf_op jit(solution)/shard_map/pallas_call | solution.py:169
  50.7 0.6 collective-permute-done.2
  51.3 0.2 add_convert_fusion
  51.5 14.4 %all_to_all.16 = bf16[32,72,128]{2,1,0:T(8,128)(2,1)S(1)} all-to-all(bf16[32,72,128]{2,1,0:T(8,128)(2,1)S(1)} %bitcast.29), channel_id=1, replica_groups=mesh['zo'=8,'zi'=2,'y'=4,'x'=4,'c'=2] {'zi','y','x'}, dimensions={0} | all-to-all | bytes 1179648 | tf_op jit(solution)/shard_map/all_to_all | solution.py:238
  65.9 0.1 convert_reduce_fusion
  66.0 0.1 select_reduce_fusion
  66.1 1.3 %collective-permute-start.3 = (f32[72,128]{1,0:T(8,128)S(1)}, f32[72,128]{1,0:T(8,128)S(1)}, u32[]{:S(2)}, u32[]{:S(2)}) collective-permute-start(f32[72,128]{1,0:T(8,128)S(1)} %get-tuple-element.10), channel_id=1, source_target_pairs={{64,0},{96,32},{128,64},{160,96},{192,128},{224,160},{256,192},{28... | collective-permute-start | bytes 110600 | tf_op jit(solution)/shard_map/ppermute | solution.py:245
  67.4 3.9 %shard_map.80 = (bf16[8,576,128]{2,1,0:T(8,128)(2,1)}, f32[72,128]{1,0:T(8,128)S(1)}) custom-call(s32[19]{0:T(128)S(1)} %pad_add_fusion.meta, bf16[8,576,128]{2,1,0:T(8,128)(2,1)S(1)} %bitcast.23, bf16[8,576,128]{2,1,0:T(8,128)(2,1)} %collective-permute-done.1.kt_ref.other_ref, bf16[1024,1024]{1,0:T(8,128)(2,1)S(1)} %get-tuple-element.6.g_ref, ...), custom_call_target="tpu_custom_call" | custom-call | flops 1207959552 | bytes 8388608 | tf_op jit(solution)/shard_map/pallas_call | solution.py:169
  71.3 2.2 %collective-permute-done.3 = f32[72,128]{1,0:T(8,128)S(1)} collective-permute-done((f32[72,128]{1,0:T(8,128)S(1)}, f32[72,128]{1,0:T(8,128)S(1)}, u32[]{:S(2)}, u32[]{:S(2)}) %collective-permute-start.3) | collective-permute-done | bytes 36896 | tf_op jit(solution)/shard_map/ppermute | solution.py:245
  73.6 11.0 %all_to_all.17 = bf16[8,72,128]{2,1,0:T(8,128)(2,1)S(1)} all-to-all(bf16[8,72,128]{2,1,0:T(8,128)(2,1)S(1)} %broadcast_in_dim.52), channel_id=1, replica_groups=mesh['zo'=8,'zi'=2,'y'=4,'x'=4,'c'=2] {'c','x'}, dimensions={0} | all-to-all | bytes 294912 | tf_op jit(solution)/shard_map/all_to_all | solution.py:263
  84.6 0.7 copy.9
  (3 shorter events, 0.0 us)
Async XLA Ops:
  1.4 6.8 %collective-permute-start = (bf16[144,128]{1,0:T(8,128)(2,1)S(1)}, bf16[144,128]{1,0:T(8,128)(2,1)S(1)}, u32[]{:S(2)}, u32[]{:S(2)}) collective-permute-start(bf16[144,128]{1,0:T(8,128)(2,1)S(1)} %fusion), channel_id=1, source_target_pairs={{0,64},{32,96},{64,128},{96,160},{128,192},{160,224},{192,256},{22... | collective-permute-start | bytes 110600 | tf_op jit(solution)/shard_map/ppermute | solution.py:192
  8.5 30.3 %copy-start.3 = (s32[16]{0:T(128)S(1)}, s32[16]{0:T(128)}, u32[]{:S(2)}) copy-start(s32[16]{0:T(128)} %param.11) | copy-start | bytes 196
  8.5 30.4 %copy-start = (bf16[128,8,576]{0,2,1:T(8,128)(2,1)S(1)}, bf16[128,8,576]{0,2,1:T(8,128)(2,1)}, u32[]{:S(2)}) copy-start(bf16[128,8,576]{0,2,1:T(8,128)(2,1)} %param.6) | copy-start | bytes 3538948
  8.5 30.4 %copy-start.1 = (bf16[128,8,576]{0,2,1:T(8,128)(2,1)S(1)}, bf16[128,8,576]{0,2,1:T(8,128)(2,1)}, u32[]{:S(2)}) copy-start(bf16[128,8,576]{0,2,1:T(8,128)(2,1)} %param.7) | copy-start | bytes 3538948
  8.5 30.4 %copy-start.2 = (f32[128,8]{0,1:T(8,128)S(1)}, f32[128,8]{0,1:T(8,128)}, u32[]{:S(2)}) copy-start(f32[128,8]{0,1:T(8,128)} %param.10) | copy-start | bytes 12292
  33.9 8.3 %collective-permute-start.1 = (bf16[8,576,128]{2,1,0:T(8,128)(2,1)S(1)}, bf16[8,576,128]{2,1,0:T(8,128)(2,1)}, u32[]{:S(2)}, u32[]{:S(2)}) collective-permute-start(bf16[8,576,128]{2,1,0:T(8,128)(2,1)S(1)} %bitcast.21), channel_id=1, source_target_pairs={{0,1},{1,0},{2,3},{3,2},{4,5},{5,4},{6,7},{7,6},{8,9},{9,8},{10,11... | collective-permute-start | bytes 3538952 | tf_op jit(solution)/shard_map/ppermute | solution.py:198
  47.4 3.9 %collective-permute-start.2 = (bf16[8,288,128]{2,1,0:T(8,128)(2,1)S(1)}, bf16[8,288,128]{2,1,0:T(8,128)(2,1)S(1)}, u32[]{:S(2)}, u32[]{:S(2)}) collective-permute-start(bf16[8,288,128]{2,1,0:T(8,128)(2,1)S(1)} %get-tuple-element.7), channel_id=1, source_target_pairs={{0,1},{1,0},{2,3},{3,2},{4,5},{5,4},{6,7},{7,6},{8,9},{9,8},{10,11... | collective-permute-start | bytes 1769480 | tf_op jit(solution)/shard_map/ppermute | solution.py:226
  66.1 7.4 %collective-permute-start.3 = (f32[72,128]{1,0:T(8,128)S(1)}, f32[72,128]{1,0:T(8,128)S(1)}, u32[]{:S(2)}, u32[]{:S(2)}) collective-permute-start(f32[72,128]{1,0:T(8,128)S(1)} %get-tuple-element.10), channel_id=1, source_target_pairs={{64,0},{96,32},{128,64},{160,96},{192,128},{224,160},{256,192},{28... | collective-permute-start | bytes 110600 | tf_op jit(solution)/shard_map/ppermute | solution.py:245

commit v4 on v3

--- a/solution.py
+++ b/solution.py
@@ -1,3 +1,4 @@
+import functools
 import math
 
 import jax
@@ -22,34 +23,35 @@
 HIDDEN = -1e30
 
 
-def key_rows(kt_ref, k_ref):
-    for j in range(SEQ_GROUP):
-        k_ref[j * TOK : (j + 1) * TOK, :] = kt_ref[j].T
-
-
-def hidden_bias(meta, bias_ref):
-    me, seq = meta[1], meta[2]
-    query_pos = seq * TOK + lax.broadcasted_iota(jnp.int32, (1, TOK), 1)
+def document_start(meta):
+    query_pos = meta[2] * TOK + lax.broadcasted_iota(jnp.int32, (1, TOK), 1)
     start = jnp.zeros((1, TOK), jnp.int32)
     end = jnp.int32(0)
     for m in range(16):
         end = end + meta[3 + m]
         start = jnp.where(query_pos >= end, end, start)
-    row = lax.broadcasted_iota(jnp.int32, (TOK, TOK), 0)
-    for j in range(SEQ_GROUP):
-        block = seq - me + j - jnp.where(j > me, SEQ_GROUP, 0)
-        key_pos = block * TOK + row
-        seen = (key_pos >= start) & (key_pos <= query_pos)
-        bias_ref[j * TOK : (j + 1) * TOK, :] = jnp.where(seen, 0.0, HIDDEN)
+    return query_pos, start
+
+
+def key_block(meta, j, positions, kt_ref, k_ref, bias_ref):
+    me, seq = meta[1], meta[2]
+    query_pos, start = positions
+    block = seq - me + j - jnp.where(j > me, SEQ_GROUP, 0)
+    key_pos = block * TOK + lax.broadcasted_iota(jnp.int32, (TOK, TOK), 0)
+    seen = (key_pos >= start) & (key_pos <= query_pos)
+    bias_ref[BLOCKS[j], :] = jnp.where(seen, 0.0, HIDDEN)
+    k_ref[BLOCKS[j], :] = kt_ref[j].T
 
 
 def both(a, b):
     return jnp.concatenate([a, b], axis=1)
 
 
-def scores(k_ref, bias_ref, queries, s_ref):
+def scores(k_ref, bias_ref, queries, s_ref, prepare=None):
     peak = jnp.full((8, 2 * TOK), HIDDEN, jnp.float32)
-    for rows in BLOCKS:
+    for j, rows in enumerate(BLOCKS):
+        if prepare is not None:
+            prepare(j)
         bias = bias_ref[rows, :]
         s = jnp.dot(k_ref[rows, :], queries, preferred_element_type=jnp.float32)
         s = s + both(bias, bias)
@@ -58,11 +60,11 @@
     return jnp.max(peak, axis=0, keepdims=True)
 
 
-def exponentials(s_ref, peak):
+def exponentials(s_ref, peak, put):
     total = jnp.zeros((8, 2 * TOK), jnp.float32)
     for rows in BLOCKS:
         e = jnp.exp2((s_ref[rows, :] - peak) * SCALE_LOG2)
-        s_ref[rows, :] = e
+        put(rows, e)
         total = total + jnp.sum(e.reshape(TOK // 8, 8, 2 * TOK), axis=0)
     return jnp.sum(total, axis=0, keepdims=True)
 
@@ -79,19 +81,22 @@
     return weight * jnp.where(student, SCALE, -SCALE)
 
 
-def all_pairs(meta, student, kt_ref, sq_ref, tq_ref, lw_ref, k_ref, bias_ref, s_ref, use):
-    key_rows(kt_ref, k_ref)
-    hidden_bias(meta, bias_ref)
-    peak = scores(k_ref, bias_ref, pair_queries(student, sq_ref, tq_ref, 0), s_ref.at[0])
+def all_pairs(meta, student, kt_ref, sq_ref, tq_ref, lw_ref, k_ref, bias_ref, s_ref, put, use):
+    positions = document_start(meta)
+    peak = scores(
+        k_ref,
+        bias_ref,
+        pair_queries(student, sq_ref, tq_ref, 0),
+        s_ref.at[0],
+        lambda j: key_block(meta, j, positions, kt_ref, k_ref, bias_ref),
+    )
     for i in range(PAIRS):
         later = None
         if i + 1 < PAIRS:
             queries = pair_queries(student, sq_ref, tq_ref, i + 1)
             later = scores(k_ref, bias_ref, queries, s_ref.at[(i + 1) % 2])
-        total = exponentials(s_ref.at[i % 2], peak)
-        factor = pair_weight(lw_ref, i, student) / total
-        for rows in BLOCKS:
-            use(i, rows, s_ref[i % 2, rows, :] * factor)
+        total = exponentials(s_ref.at[i % 2], peak, functools.partial(put, i))
+        use(i, pair_weight(lw_ref, i, student) / total)
         peak = later
 
 
@@ -99,12 +104,15 @@
     return slice(i * 2 * TOK, (i + 1) * 2 * TOK)
 
 
-def first_kernel(meta, kt_ref, sq_ref, tq_ref, lw_ref, p_ref, k_ref, bias_ref, s_ref):
-    def use(i, rows, probs):
-        p_ref[rows, pair_lanes(i)] = probs
+def first_kernel(meta, kt_ref, sq_ref, tq_ref, lw_ref, e_ref, k_ref, bias_ref, s_ref):
+    def put(i, rows, e):
+        e_ref[rows, pair_lanes(i)] = e
+
+    def use(i, factor):
+        e_ref[WIN : WIN + 1, pair_lanes(i)] = factor
 
     student = meta[0] == 0
-    all_pairs(meta, student, kt_ref, sq_ref, tq_ref, lw_ref, k_ref, bias_ref, s_ref, use)
+    all_pairs(meta, student, kt_ref, sq_ref, tq_ref, lw_ref, k_ref, bias_ref, s_ref, put, use)
 
 
 def key_grad_half(sq_ref, half, g):
@@ -116,14 +124,21 @@
 
 
 def second_kernel(
-    meta, kt_ref, sq_ref, tq_ref, lw_ref, p_ref, g_ref, kg_ref, k_ref, bias_ref, s_ref
+    meta, kt_ref, sq_ref, tq_ref, lw_ref, e_ref, g_ref, kg_ref, k_ref, bias_ref, s_ref
 ):
     student = meta[0] == 1
 
-    def use(i, rows, probs):
-        g_ref[rows, pair_lanes(i)] = (p_ref[rows, pair_lanes(i)] + probs).astype(jnp.bfloat16)
-
-    all_pairs(meta, student, kt_ref, sq_ref, tq_ref, lw_ref, k_ref, bias_ref, s_ref, use)
+    def put(i, rows, e):
+        s_ref[i % 2, rows, :] = e
+
+    def use(i, factor):
+        lanes = pair_lanes(i)
+        first = e_ref[WIN : WIN + 1, lanes]
+        for rows in BLOCKS:
+            g = e_ref[rows, lanes] * first + s_ref[i % 2, rows, :] * factor
+            g_ref[rows, lanes] = g.astype(jnp.bfloat16)
+
+    all_pairs(meta, student, kt_ref, sq_ref, tq_ref, lw_ref, k_ref, bias_ref, s_ref, put, use)
     grad = key_grad_half(sq_ref, 1 - meta[0], g_ref[...]).astype(jnp.bfloat16)
     for j in range(SEQ_GROUP):
         kg_ref[j] = grad[:, j * TOK : (j + 1) * TOK]
@@ -204,10 +219,10 @@
         pltpu.VMEM((2, WIN, 2 * TOK), jnp.float32),
     ]
     matmul = 2 * WIN * HEADS * TOK * KDIM
-    probs = call(
+    first = call(
         first_kernel,
         in_vmem,
-        jax.ShapeDtypeStruct((WIN, HEADS * TOK), jnp.float32),
+        jax.ShapeDtypeStruct((WIN + 8, HEADS * TOK), jnp.float32),
         scratch,
         12,
         matmul,
@@ -221,7 +236,7 @@
         scratch,
         12,
         matmul * 3 // 2,
-        (meta, other, sq, tq, lw, probs),
+        (meta, other, sq, tq, lw, first),
     )
     got = lax.ppermute(sent, "c", [(0, 1), (1, 0)])
     own_half = call(

time: 85.8 us -> 85.1 us (level)
  transfers between devices with their start and end apart: 4 -> 4, of which waited for: 3 -> 3; matrix products, arithmetic and copies ran while one was open for 0% -> 0% of each run, Pallas kernels for 10% -> 9%
where the time goes in v4:
time: 85.1 us; the launch traced here: 84.6 us
  blocking collectives  50.8 us (60%)
  starting transfers between devices  14 us (16%)
  Pallas kernels  13 us (15%)
  waiting for transfers between devices  3.75 us (4%)
  other arithmetic  1.33 us (2%)
  local copies, waits for them, and re-layouts  0.86 us (1%)
    all_to_all x1, blocking collectives, on_device(): lax.all_to_all(outgoing.reshape(SEQ_GROUP * 4, PIECE, TOK), ('zi', 'y', '...  25.4 us
    all_to_all x1, blocking collectives, on_device(): lax.all_to_all(partial.reshape(SEQ_GROUP * 4, rows, TOK), ('zi', 'y', 'x'...  14.4 us
    pallas_call x4, Pallas kernels, call(): pl.pallas_call(kernel, in_specs=[pl.BlockSpec(memory_space=pltpu.SMEM)] +...  13 us
    all_to_all x1, blocking collectives, on_device(): lax.all_to_all(jnp.broadcast_to(share, (8, rows, TOK)), ('c', 'x'), 0, 0,...  11 us
    ppermute x1, starting transfers between devices, on_device(): before = lax.ppermute(own, ('zo', 'zi'), [(i, i + 2) for i in range(14)])  5.73 us
    ppermute x1, starting transfers between devices, on_device(): other = lax.ppermute(mine, 'c', [(0, 1), (1, 0)])  4.9 us
    ppermute x1, waiting for transfers between devices, on_device(): lax.ppermute(returned, ('zo', 'zi'), [(i + 2, i) for i in range(14)])  2.23 us
    ppermute x1, starting transfers between devices, on_device(): got = lax.ppermute(sent, 'c', [(0, 1), (1, 0)])  2.04 us
  transfers between devices with their start and end apart: 4, of which 3 were waited for; matrix products, arithmetic and copies ran while one was open for 0% of the time, Pallas kernels for 9%

profile of v4, /device:TPU:1, one launch (start us, length us, event | category | flops | bytes accessed | tf_op | source)
XLA Modules:
  0.0 84.6 jit_solution(8026014800209253131)
XLA Ops:
  0.6 0.8 fusion
  1.4 5.7 %collective-permute-start = (bf16[144,128]{1,0:T(8,128)(2,1)S(1)}, bf16[144,128]{1,0:T(8,128)(2,1)S(1)}, u32[]{:S(2)}, u32[]{:S(2)}) collective-permute-start(bf16[144,128]{1,0:T(8,128)(2,1)S(1)} %fusion), channel_id=1, source_target_pairs={{0,64},{32,96},{64,128},{96,160},{128,192},{160,224},{192,256},{22... | collective-permute-start | bytes 110600 | tf_op jit(solution)/shard_map/ppermute | solution.py:207
  7.2 1.0 %collective-permute-done = bf16[144,128]{1,0:T(8,128)(2,1)S(1)} collective-permute-done((bf16[144,128]{1,0:T(8,128)(2,1)S(1)}, bf16[144,128]{1,0:T(8,128)(2,1)S(1)}, u32[]{:S(2)}, u32[]{:S(2)}) %collective-permute-start) | collective-permute-done | bytes 36896 | tf_op jit(solution)/shard_map/ppermute | solution.py:207
  8.2 0.1 broadcast_select_fusion
  8.3 0.2 broadcast_in_dim.49
  8.5 0.0 copy-start.3
  8.5 0.0 copy-start
  8.5 0.0 copy-start.1
  8.5 0.0 copy-start.2
  8.5 25.4 %all_to_all.15 = bf16[32,144,128]{2,1,0:T(8,128)(2,1)S(1)} all-to-all(bf16[32,144,128]{2,1,0:T(8,128)(2,1)S(1)} %bitcast.28), channel_id=1, replica_groups=mesh['zo'=8,'zi'=2,'y'=4,'x'=4,'c'=2] {'zi','y','x'}, dimensions={0} | all-to-all | bytes 2359296 | tf_op jit(solution)/shard_map/all_to_all | solution.py:210
  33.9 4.9 %collective-permute-start.1 = (bf16[8,576,128]{2,1,0:T(8,128)(2,1)S(1)}, bf16[8,576,128]{2,1,0:T(8,128)(2,1)}, u32[]{:S(2)}, u32[]{:S(2)}) collective-permute-start(bf16[8,576,128]{2,1,0:T(8,128)(2,1)S(1)} %bitcast.21), channel_id=1, source_target_pairs={{0,1},{1,0},{2,3},{3,2},{4,5},{5,4},{6,7},{7,6},{8,9},{9,8},{10,11... | collective-permute-start | bytes 3538952 | tf_op jit(solution)/shard_map/ppermute | solution.py:213
  38.8 0.0 copy-done.3
  38.8 0.1 pad_add_fusion.meta
  38.9 0.0 copy-done
  38.9 0.0 copy-done.1
  38.9 0.0 copy-done.2
  38.9 2.7 %shard_map.77.e_ref = f32[1032,1024]{1,0:T(8,128)S(1)} custom-call(s32[19]{0:T(128)S(1)} %pad_add_fusion.meta, bf16[8,576,128]{2,1,0:T(8,128)(2,1)S(1)} %bitcast.22, bf16[8,576,128]{2,1,0:T(8,128)(2,1)S(1)} %bitcast.18, bf16[8,576,128]{2,1,0:T(8,128)(2,1)S(1)} %bitcast.24, f32[8,128]{1,0:T(8,128)S(1)} %bitcast.26), custom_call_target="tpu_custom_call" | custom-call | flops 1207959552 | bytes 8388608 | tf_op jit(solution)/shard_map/pallas_call | solution.py:184
  41.6 0.0 collective-permute-done.1.kt_ref.other_ref
  41.6 5.1 %shard_map.78 = (bf16[1024,1024]{1,0:T(8,128)(2,1)S(1)}, bf16[8,288,128]{2,1,0:T(8,128)(2,1)S(1)}) custom-call(s32[19]{0:T(128)S(1)} %pad_add_fusion.meta, bf16[8,576,128]{2,1,0:T(8,128)(2,1)} %collective-permute-done.1.kt_ref.other_ref, bf16[8,576,128]{2,1,0:T(8,128)(2,1)S(1)} %bitcast.19, bf16[8,576,128]{2,1,0:T(8,128)(2,1)S(1)} %bitcast.25, ...), custom_call_target="tpu_custom_call" | custom-call | flops 1811939328 | bytes 8388608 | tf_op jit(solution)/shard_map/pallas_call | solution.py:184
  46.7 2.0 %collective-permute-start.2 = (bf16[8,288,128]{2,1,0:T(8,128)(2,1)S(1)}, bf16[8,288,128]{2,1,0:T(8,128)(2,1)S(1)}, u32[]{:S(2)}, u32[]{:S(2)}) collective-permute-start(bf16[8,288,128]{2,1,0:T(8,128)(2,1)S(1)} %get-tuple-element.7), channel_id=1, source_target_pairs={{0,1},{1,0},{2,3},{3,2},{4,5},{5,4},{6,7},{7,6},{8,9},{9,8},{10,11... | collective-permute-start | bytes 1769480 | tf_op jit(solution)/shard_map/ppermute | solution.py:241
  48.8 1.3 %shard_map.79 = f32[8,288,128]{2,1,0:T(8,128)S(1)} custom-call(s32[19]{0:T(128)S(1)} %pad_add_fusion.meta, bf16[8,576,128]{2,1,0:T(8,128)(2,1)S(1)} %bitcast.20, bf16[1024,1024]{1,0:T(8,128)(2,1)S(1)} %get-tuple-element.6.g_ref), custom_call_target="tpu_custom_call" | custom-call | flops 603979776 | bytes 8388608 | tf_op jit(solution)/shard_map/pallas_call | solution.py:184
  50.1 0.5 collective-permute-done.2
  50.6 0.2 add_convert_fusion
  50.8 14.4 %all_to_all.16 = bf16[32,72,128]{2,1,0:T(8,128)(2,1)S(1)} all-to-all(bf16[32,72,128]{2,1,0:T(8,128)(2,1)S(1)} %bitcast.29), channel_id=1, replica_groups=mesh['zo'=8,'zi'=2,'y'=4,'x'=4,'c'=2] {'zi','y','x'}, dimensions={0} | all-to-all | bytes 1179648 | tf_op jit(solution)/shard_map/all_to_all | solution.py:253
  65.2 0.1 convert_reduce_fusion
  65.3 0.1 select_reduce_fusion
  65.4 1.3 %collective-permute-start.3 = (f32[72,128]{1,0:T(8,128)S(1)}, f32[72,128]{1,0:T(8,128)S(1)}, u32[]{:S(2)}, u32[]{:S(2)}) collective-permute-start(f32[72,128]{1,0:T(8,128)S(1)} %get-tuple-element.10), channel_id=1, source_target_pairs={{64,0},{96,32},{128,64},{160,96},{192,128},{224,160},{256,192},{28... | collective-permute-start | bytes 110600 | tf_op jit(solution)/shard_map/ppermute | solution.py:260
  66.7 3.9 %shard_map.80 = (bf16[8,576,128]{2,1,0:T(8,128)(2,1)}, f32[72,128]{1,0:T(8,128)S(1)}) custom-call(s32[19]{0:T(128)S(1)} %pad_add_fusion.meta, bf16[8,576,128]{2,1,0:T(8,128)(2,1)S(1)} %bitcast.23, bf16[8,576,128]{2,1,0:T(8,128)(2,1)} %collective-permute-done.1.kt_ref.other_ref, bf16[1024,1024]{1,0:T(8,128)(2,1)S(1)} %get-tuple-element.6.g_ref, ...), custom_call_target="tpu_custom_call" | custom-call | flops 1207959552 | bytes 8388608 | tf_op jit(solution)/shard_map/pallas_call | solution.py:184
  70.6 2.2 %collective-permute-done.3 = f32[72,128]{1,0:T(8,128)S(1)} collective-permute-done((f32[72,128]{1,0:T(8,128)S(1)}, f32[72,128]{1,0:T(8,128)S(1)}, u32[]{:S(2)}, u32[]{:S(2)}) %collective-permute-start.3) | collective-permute-done | bytes 36896 | tf_op jit(solution)/shard_map/ppermute | solution.py:260
  72.9 11.0 %all_to_all.17 = bf16[8,72,128]{2,1,0:T(8,128)(2,1)S(1)} all-to-all(bf16[8,72,128]{2,1,0:T(8,128)(2,1)S(1)} %broadcast_in_dim.52), channel_id=1, replica_groups=mesh['zo'=8,'zi'=2,'y'=4,'x'=4,'c'=2] {'c','x'}, dimensions={0} | all-to-all | bytes 294912 | tf_op jit(solution)/shard_map/all_to_all | solution.py:278
  83.9 0.7 copy.9
  (3 shorter events, 0.0 us)
Async XLA Ops:
  1.4 6.8 %collective-permute-start = (bf16[144,128]{1,0:T(8,128)(2,1)S(1)}, bf16[144,128]{1,0:T(8,128)(2,1)S(1)}, u32[]{:S(2)}, u32[]{:S(2)}) collective-permute-start(bf16[144,128]{1,0:T(8,128)(2,1)S(1)} %fusion), channel_id=1, source_target_pairs={{0,64},{32,96},{64,128},{96,160},{128,192},{160,224},{192,256},{22... | collective-permute-start | bytes 110600 | tf_op jit(solution)/shard_map/ppermute | solution.py:207
  8.5 30.3 %copy-start.3 = (s32[16]{0:T(128)S(1)}, s32[16]{0:T(128)}, u32[]{:S(2)}) copy-start(s32[16]{0:T(128)} %param.11) | copy-start | bytes 196
  8.5 30.4 %copy-start = (bf16[128,8,576]{0,2,1:T(8,128)(2,1)S(1)}, bf16[128,8,576]{0,2,1:T(8,128)(2,1)}, u32[]{:S(2)}) copy-start(bf16[128,8,576]{0,2,1:T(8,128)(2,1)} %param.6) | copy-start | bytes 3538948
  8.5 30.4 %copy-start.1 = (bf16[128,8,576]{0,2,1:T(8,128)(2,1)S(1)}, bf16[128,8,576]{0,2,1:T(8,128)(2,1)}, u32[]{:S(2)}) copy-start(bf16[128,8,576]{0,2,1:T(8,128)(2,1)} %param.7) | copy-start | bytes 3538948
  8.5 30.4 %copy-start.2 = (f32[128,8]{0,1:T(8,128)S(1)}, f32[128,8]{0,1:T(8,128)}, u32[]{:S(2)}) copy-start(f32[128,8]{0,1:T(8,128)} %param.10) | copy-start | bytes 12292
  33.9 7.7 %collective-permute-start.1 = (bf16[8,576,128]{2,1,0:T(8,128)(2,1)S(1)}, bf16[8,576,128]{2,1,0:T(8,128)(2,1)}, u32[]{:S(2)}, u32[]{:S(2)}) collective-permute-start(bf16[8,576,128]{2,1,0:T(8,128)(2,1)S(1)} %bitcast.21), channel_id=1, source_target_pairs={{0,1},{1,0},{2,3},{3,2},{4,5},{5,4},{6,7},{7,6},{8,9},{9,8},{10,11... | collective-permute-start | bytes 3538952 | tf_op jit(solution)/shard_map/ppermute | solution.py:213
  46.7 3.9 %collective-permute-start.2 = (bf16[8,288,128]{2,1,0:T(8,128)(2,1)S(1)}, bf16[8,288,128]{2,1,0:T(8,128)(2,1)S(1)}, u32[]{:S(2)}, u32[]{:S(2)}) collective-permute-start(bf16[8,288,128]{2,1,0:T(8,128)(2,1)S(1)} %get-tuple-element.7), channel_id=1, source_target_pairs={{0,1},{1,0},{2,3},{3,2},{4,5},{5,4},{6,7},{7,6},{8,9},{9,8},{10,11... | collective-permute-start | bytes 1769480 | tf_op jit(solution)/shard_map/ppermute | solution.py:241
  65.4 7.4 %collective-permute-start.3 = (f32[72,128]{1,0:T(8,128)S(1)}, f32[72,128]{1,0:T(8,128)S(1)}, u32[]{:S(2)}, u32[]{:S(2)}) collective-permute-start(f32[72,128]{1,0:T(8,128)S(1)} %get-tuple-element.10), channel_id=1, source_target_pairs={{64,0},{96,32},{128,64},{160,96},{192,128},{224,160},{256,192},{28... | collective-permute-start | bytes 110600 | tf_op jit(solution)/shard_map/ppermute | solution.py:260

commit v5 on v4

--- a/solution.py
+++ b/solution.py
@@ -257,7 +257,7 @@
     here = (jnp.arange(SEQ_GROUP) >= me)[:, None, None]
     kept = jnp.sum(jnp.where(here, terms, 0.0), axis=0)
     returned = jnp.sum(jnp.where(here, 0.0, terms), axis=0)
-    returned = lax.ppermute(returned, ("zo", "zi"), [(i + 2, i) for i in range(14)])
+    returned = lax.ppermute(returned.astype(jnp.bfloat16), ("zo", "zi"), [(i + 2, i) for i in range(14)])
     query_grad, kept = call(
         query_kernel,
         [pl.BlockSpec(memory_space=pl.ANY), in_vmem],
@@ -274,7 +274,7 @@
         matmul,
         (meta, mine, other, score_grad, kept),
     )
-    share = (kept + returned).astype(jnp.bfloat16)
+    share = (kept + returned.astype(jnp.float32)).astype(jnp.bfloat16)
     key_grad = lax.all_to_all(
         jnp.broadcast_to(share, (8, rows, TOK)), ("c", "x"), 0, 0, tiled=True
     ).reshape(KDIM, TOK)

time: 85.1 us -> 84.9 us (level)
  no operation moved by 1% of the time
where the time goes in v5:
time: 84.9 us; the launch traced here: 84.4 us
  blocking collectives  50.8 us (60%)
  starting transfers between devices  14 us (16%)
  Pallas kernels  13 us (15%)
  waiting for transfers between devices  3.55 us (4%)
  other arithmetic  1.33 us (2%)
  local copies, waits for them, and re-layouts  0.86 us (1%)
    all_to_all x1, blocking collectives, on_device(): lax.all_to_all(outgoing.reshape(SEQ_GROUP * 4, PIECE, TOK), ('zi', 'y', '...  25.4 us
    all_to_all x1, blocking collectives, on_device(): lax.all_to_all(partial.reshape(SEQ_GROUP * 4, rows, TOK), ('zi', 'y', 'x'...  14.4 us
    pallas_call x4, Pallas kernels, call(): pl.pallas_call(kernel, in_specs=[pl.BlockSpec(memory_space=pltpu.SMEM)] +...  13 us
    all_to_all x1, blocking collectives, on_device(): lax.all_to_all(jnp.broadcast_to(share, (8, rows, TOK)), ('c', 'x'), 0, 0,...  11 us
    ppermute x1, starting transfers between devices, on_device(): before = lax.ppermute(own, ('zo', 'zi'), [(i, i + 2) for i in range(14)])  5.73 us
    ppermute x1, starting transfers between devices, on_device(): other = lax.ppermute(mine, 'c', [(0, 1), (1, 0)])  4.9 us
    ppermute x1, starting transfers between devices, on_device(): got = lax.ppermute(sent, 'c', [(0, 1), (1, 0)])  2.04 us
    ppermute x1, waiting for transfers between devices, on_device(): lax.ppermute(returned.astype(jnp.bfloat16), ('zo', 'zi'), [(i + 2, i) for...  2.03 us
  transfers between devices with their start and end apart: 4, of which 3 were waited for; matrix products, arithmetic and copies ran while one was open for 0% of the time, Pallas kernels for 9%

profile of v5, /device:TPU:1, one launch (start us, length us, event | category | flops | bytes accessed | tf_op | source)
XLA Modules:
  0.0 84.4 jit_solution(3107101356619148855)
XLA Ops:
  0.6 0.8 fusion
  1.4 5.7 %collective-permute-start = (bf16[144,128]{1,0:T(8,128)(2,1)S(1)}, bf16[144,128]{1,0:T(8,128)(2,1)S(1)}, u32[]{:S(2)}, u32[]{:S(2)}) collective-permute-start(bf16[144,128]{1,0:T(8,128)(2,1)S(1)} %fusion), channel_id=1, source_target_pairs={{0,64},{32,96},{64,128},{96,160},{128,192},{160,224},{192,256},{22... | collective-permute-start | bytes 110600 | tf_op jit(solution)/shard_map/ppermute | solution.py:207
  7.2 1.0 %collective-permute-done = bf16[144,128]{1,0:T(8,128)(2,1)S(1)} collective-permute-done((bf16[144,128]{1,0:T(8,128)(2,1)S(1)}, bf16[144,128]{1,0:T(8,128)(2,1)S(1)}, u32[]{:S(2)}, u32[]{:S(2)}) %collective-permute-start) | collective-permute-done | bytes 36896 | tf_op jit(solution)/shard_map/ppermute | solution.py:207
  8.2 0.1 broadcast_select_fusion
  8.3 0.2 broadcast_in_dim.49
  8.5 0.0 copy-start.3
  8.5 0.0 copy-start
  8.5 0.0 copy-start.1
  8.5 0.0 copy-start.2
  8.5 25.4 %all_to_all.15 = bf16[32,144,128]{2,1,0:T(8,128)(2,1)S(1)} all-to-all(bf16[32,144,128]{2,1,0:T(8,128)(2,1)S(1)} %bitcast.28), channel_id=1, replica_groups=mesh['zo'=8,'zi'=2,'y'=4,'x'=4,'c'=2] {'zi','y','x'}, dimensions={0} | all-to-all | bytes 2359296 | tf_op jit(solution)/shard_map/all_to_all | solution.py:210
  33.9 4.9 %collective-permute-start.1 = (bf16[8,576,128]{2,1,0:T(8,128)(2,1)S(1)}, bf16[8,576,128]{2,1,0:T(8,128)(2,1)}, u32[]{:S(2)}, u32[]{:S(2)}) collective-permute-start(bf16[8,576,128]{2,1,0:T(8,128)(2,1)S(1)} %bitcast.21), channel_id=1, source_target_pairs={{0,1},{1,0},{2,3},{3,2},{4,5},{5,4},{6,7},{7,6},{8,9},{9,8},{10,11... | collective-permute-start | bytes 3538952 | tf_op jit(solution)/shard_map/ppermute | solution.py:213
  38.8 0.0 copy-done.3
  38.8 0.1 pad_add_fusion.meta
  38.9 0.0 copy-done
  38.9 0.0 copy-done.1
  38.9 0.0 copy-done.2
  38.9 2.7 %shard_map.77.e_ref = f32[1032,1024]{1,0:T(8,128)S(1)} custom-call(s32[19]{0:T(128)S(1)} %pad_add_fusion.meta, bf16[8,576,128]{2,1,0:T(8,128)(2,1)S(1)} %bitcast.22, bf16[8,576,128]{2,1,0:T(8,128)(2,1)S(1)} %bitcast.18, bf16[8,576,128]{2,1,0:T(8,128)(2,1)S(1)} %bitcast.24, f32[8,128]{1,0:T(8,128)S(1)} %bitcast.26), custom_call_target="tpu_custom_call" | custom-call | flops 1207959552 | bytes 8388608 | tf_op jit(solution)/shard_map/pallas_call | solution.py:184
  41.6 0.0 collective-permute-done.1.kt_ref.other_ref
  41.6 5.1 %shard_map.78 = (bf16[1024,1024]{1,0:T(8,128)(2,1)S(1)}, bf16[8,288,128]{2,1,0:T(8,128)(2,1)S(1)}) custom-call(s32[19]{0:T(128)S(1)} %pad_add_fusion.meta, bf16[8,576,128]{2,1,0:T(8,128)(2,1)} %collective-permute-done.1.kt_ref.other_ref, bf16[8,576,128]{2,1,0:T(8,128)(2,1)S(1)} %bitcast.19, bf16[8,576,128]{2,1,0:T(8,128)(2,1)S(1)} %bitcast.25, ...), custom_call_target="tpu_custom_call" | custom-call | flops 1811939328 | bytes 8388608 | tf_op jit(solution)/shard_map/pallas_call | solution.py:184
  46.7 2.0 %collective-permute-start.2 = (bf16[8,288,128]{2,1,0:T(8,128)(2,1)S(1)}, bf16[8,288,128]{2,1,0:T(8,128)(2,1)S(1)}, u32[]{:S(2)}, u32[]{:S(2)}) collective-permute-start(bf16[8,288,128]{2,1,0:T(8,128)(2,1)S(1)} %get-tuple-element.7), channel_id=1, source_target_pairs={{0,1},{1,0},{2,3},{3,2},{4,5},{5,4},{6,7},{7,6},{8,9},{9,8},{10,11... | collective-permute-start | bytes 1769480 | tf_op jit(solution)/shard_map/ppermute | solution.py:241
  48.8 1.3 %shard_map.79 = f32[8,288,128]{2,1,0:T(8,128)S(1)} custom-call(s32[19]{0:T(128)S(1)} %pad_add_fusion.meta, bf16[8,576,128]{2,1,0:T(8,128)(2,1)S(1)} %bitcast.20, bf16[1024,1024]{1,0:T(8,128)(2,1)S(1)} %get-tuple-element.6.g_ref), custom_call_target="tpu_custom_call" | custom-call | flops 603979776 | bytes 8388608 | tf_op jit(solution)/shard_map/pallas_call | solution.py:184
  50.1 0.5 collective-permute-done.2
  50.6 0.2 add_convert_fusion
  50.8 14.4 %all_to_all.16 = bf16[32,72,128]{2,1,0:T(8,128)(2,1)S(1)} all-to-all(bf16[32,72,128]{2,1,0:T(8,128)(2,1)S(1)} %bitcast.29), channel_id=1, replica_groups=mesh['zo'=8,'zi'=2,'y'=4,'x'=4,'c'=2] {'zi','y','x'}, dimensions={0} | all-to-all | bytes 1179648 | tf_op jit(solution)/shard_map/all_to_all | solution.py:253
  65.2 0.1 convert_reduce_fusion
  65.3 0.1 select_reduce_fusion
  65.4 1.3 %collective-permute-start.3 = (bf16[72,128]{1,0:T(8,128)(2,1)S(1)}, bf16[72,128]{1,0:T(8,128)(2,1)S(1)}, u32[]{:S(2)}, u32[]{:S(2)}) collective-permute-start(bf16[72,128]{1,0:T(8,128)(2,1)S(1)} %get-tuple-element.10), channel_id=1, source_target_pairs={{64,0},{96,32},{128,64},{160,96},{192,128},{224,160},{256,192},{28... | collective-permute-start | bytes 55304 | tf_op jit(solution)/shard_map/ppermute | solution.py:260
  66.7 3.9 %shard_map.80 = (bf16[8,576,128]{2,1,0:T(8,128)(2,1)}, f32[72,128]{1,0:T(8,128)S(1)}) custom-call(s32[19]{0:T(128)S(1)} %pad_add_fusion.meta, bf16[8,576,128]{2,1,0:T(8,128)(2,1)S(1)} %bitcast.23, bf16[8,576,128]{2,1,0:T(8,128)(2,1)} %collective-permute-done.1.kt_ref.other_ref, bf16[1024,1024]{1,0:T(8,128)(2,1)S(1)} %get-tuple-element.6.g_ref, ...), custom_call_target="tpu_custom_call" | custom-call | flops 1207959552 | bytes 8388608 | tf_op jit(solution)/shard_map/pallas_call | solution.py:184
  70.6 2.0 %collective-permute-done.3 = bf16[72,128]{1,0:T(8,128)(2,1)S(1)} collective-permute-done((bf16[72,128]{1,0:T(8,128)(2,1)S(1)}, bf16[72,128]{1,0:T(8,128)(2,1)S(1)}, u32[]{:S(2)}, u32[]{:S(2)}) %collective-permute-start.3) | collective-permute-done | bytes 18464 | tf_op jit(solution)/shard_map/ppermute | solution.py:260
  72.7 11.0 %all_to_all.17 = bf16[8,72,128]{2,1,0:T(8,128)(2,1)S(1)} all-to-all(bf16[8,72,128]{2,1,0:T(8,128)(2,1)S(1)} %broadcast_in_dim.52), channel_id=1, replica_groups=mesh['zo'=8,'zi'=2,'y'=4,'x'=4,'c'=2] {'c','x'}, dimensions={0} | all-to-all | bytes 294912 | tf_op jit(solution)/shard_map/all_to_all | solution.py:278
  83.7 0.7 copy.9
  (3 shorter events, 0.0 us)
Async XLA Ops:
  1.4 6.8 %collective-permute-start = (bf16[144,128]{1,0:T(8,128)(2,1)S(1)}, bf16[144,128]{1,0:T(8,128)(2,1)S(1)}, u32[]{:S(2)}, u32[]{:S(2)}) collective-permute-start(bf16[144,128]{1,0:T(8,128)(2,1)S(1)} %fusion), channel_id=1, source_target_pairs={{0,64},{32,96},{64,128},{96,160},{128,192},{160,224},{192,256},{22... | collective-permute-start | bytes 110600 | tf_op jit(solution)/shard_map/ppermute | solution.py:207
  8.5 30.3 %copy-start.3 = (s32[16]{0:T(128)S(1)}, s32[16]{0:T(128)}, u32[]{:S(2)}) copy-start(s32[16]{0:T(128)} %param.11) | copy-start | bytes 196
  8.5 30.4 %copy-start = (bf16[128,8,576]{0,2,1:T(8,128)(2,1)S(1)}, bf16[128,8,576]{0,2,1:T(8,128)(2,1)}, u32[]{:S(2)}) copy-start(bf16[128,8,576]{0,2,1:T(8,128)(2,1)} %param.6) | copy-start | bytes 3538948
  8.5 30.4 %copy-start.1 = (bf16[128,8,576]{0,2,1:T(8,128)(2,1)S(1)}, bf16[128,8,576]{0,2,1:T(8,128)(2,1)}, u32[]{:S(2)}) copy-start(bf16[128,8,576]{0,2,1:T(8,128)(2,1)} %param.7) | copy-start | bytes 3538948
  8.5 30.4 %copy-start.2 = (f32[128,8]{0,1:T(8,128)S(1)}, f32[128,8]{0,1:T(8,128)}, u32[]{:S(2)}) copy-start(f32[128,8]{0,1:T(8,128)} %param.10) | copy-start | bytes 12292
  33.9 7.7 %collective-permute-start.1 = (bf16[8,576,128]{2,1,0:T(8,128)(2,1)S(1)}, bf16[8,576,128]{2,1,0:T(8,128)(2,1)}, u32[]{:S(2)}, u32[]{:S(2)}) collective-permute-start(bf16[8,576,128]{2,1,0:T(8,128)(2,1)S(1)} %bitcast.21), channel_id=1, source_target_pairs={{0,1},{1,0},{2,3},{3,2},{4,5},{5,4},{6,7},{7,6},{8,9},{9,8},{10,11... | collective-permute-start | bytes 3538952 | tf_op jit(solution)/shard_map/ppermute | solution.py:213
  46.7 3.9 %collective-permute-start.2 = (bf16[8,288,128]{2,1,0:T(8,128)(2,1)S(1)}, bf16[8,288,128]{2,1,0:T(8,128)(2,1)S(1)}, u32[]{:S(2)}, u32[]{:S(2)}) collective-permute-start(bf16[8,288,128]{2,1,0:T(8,128)(2,1)S(1)} %get-tuple-element.7), channel_id=1, source_target_pairs={{0,1},{1,0},{2,3},{3,2},{4,5},{5,4},{6,7},{7,6},{8,9},{9,8},{10,11... | collective-permute-start | bytes 1769480 | tf_op jit(solution)/shard_map/ppermute | solution.py:241
  65.4 7.2 %collective-permute-start.3 = (bf16[72,128]{1,0:T(8,128)(2,1)S(1)}, bf16[72,128]{1,0:T(8,128)(2,1)S(1)}, u32[]{:S(2)}, u32[]{:S(2)}) collective-permute-start(bf16[72,128]{1,0:T(8,128)(2,1)S(1)} %get-tuple-element.10), channel_id=1, source_target_pairs={{64,0},{96,32},{128,64},{160,96},{192,128},{224,160},{256,192},{28... | collective-permute-start | bytes 55304 | tf_op jit(solution)/shard_map/ppermute | solution.py:260

commit v6 on v5

--- a/solution.py
+++ b/solution.py
@@ -145,19 +145,22 @@
 
 
 def query_kernel(
-    meta, mine_ref, other_ref, g_ref, kept_ref, out_ref, kept_out_ref, kt_ref, stage_ref, sems
+    meta, mine_ref, other_ref, g_ref, kept_ref, out_ref, kept_out_ref, kt_ref, stage_ref, sems, key_sems
 ):
     kept_out_ref[...] = kept_ref[...]
 
-    @pl.when(meta[0] == 0)
-    def _():
-        for j in range(SEQ_GROUP):
-            kt_ref[:, j * TOK : (j + 1) * TOK] = mine_ref[j]
-
-    @pl.when(meta[0] == 1)
-    def _():
-        for j in range(SEQ_GROUP):
-            kt_ref[:, j * TOK : (j + 1) * TOK] = other_ref[j]
+    def fetch(keys_ref):
+        fetched = [
+            pltpu.make_async_copy(keys_ref.at[j], kt_ref.at[:, lanes], key_sems.at[j])
+            for j, lanes in enumerate(BLOCKS)
+        ]
+        for copy in fetched:
+            copy.start()
+        for copy in fetched:
+            copy.wait()
+
+    pl.when(meta[0] == 0)(lambda: fetch(mine_ref))
+    pl.when(meta[0] == 1)(lambda: fetch(other_ref))
 
     copies = []
     for i in range(PAIRS):
@@ -179,11 +182,13 @@
         out_ref[j] = grad[:, lanes]
 
 
-def call(kernel, out_specs, out_shape, scratch, mib, flops, args):
+def call(kernel, out_specs, out_shape, scratch, mib, flops, args, left=0):
     in_vmem = pl.BlockSpec(memory_space=pltpu.VMEM)
     return pl.pallas_call(
         kernel,
-        in_specs=[pl.BlockSpec(memory_space=pltpu.SMEM)] + [in_vmem] * (len(args) - 1),
+        in_specs=[pl.BlockSpec(memory_space=pltpu.SMEM)]
+        + [pl.BlockSpec(memory_space=pl.ANY)] * left
+        + [in_vmem] * (len(args) - 1 - left),
         out_specs=out_specs,
         out_shape=out_shape,
         scratch_shapes=scratch,
@@ -269,10 +274,12 @@
             pltpu.VMEM((KDIM, WIN), jnp.bfloat16),
             pltpu.VMEM((HEADS, KDIM, TOK), jnp.bfloat16),
             pltpu.SemaphoreType.DMA((PAIRS,)),
+            pltpu.SemaphoreType.DMA((SEQ_GROUP,)),
         ],
         8,
         matmul,
         (meta, mine, other, score_grad, kept),
+        left=2,
     )
     share = (kept + returned.astype(jnp.float32)).astype(jnp.bfloat16)
     key_grad = lax.all_to_all(

time: 84.9 us -> 84.9 us (level)
  transfers between devices with their start and end apart: 4 -> 4, of which waited for: 3 -> 3; matrix products, arithmetic and copies ran while one was open for 0% -> 0% of each run, Pallas kernels for 9% -> 10%
where the time goes in v6:
time: 84.9 us; the launch traced here: 84.4 us
  blocking collectives  50.8 us (60%)
  starting transfers between devices  14 us (16%)
  Pallas kernels  13.4 us (16%)
  waiting for transfers between devices  3.23 us (4%)
  other arithmetic  1.33 us (2%)
  local copies, waits for them, and re-layouts  0.86 us (1%)
    all_to_all x1, blocking collectives, on_device(): lax.all_to_all(outgoing.reshape(SEQ_GROUP * 4, PIECE, TOK), ('zi', 'y', '...  25.4 us
    all_to_all x1, blocking collectives, on_device(): lax.all_to_all(partial.reshape(SEQ_GROUP * 4, rows, TOK), ('zi', 'y', 'x'...  14.4 us
    pallas_call x4, Pallas kernels, call(): pl.pallas_call(kernel, in_specs=[pl.BlockSpec(memory_space=pltpu.SMEM)] +...  13.4 us
    all_to_all x1, blocking collectives, on_device(): lax.all_to_all(jnp.broadcast_to(share, (8, rows, TOK)), ('c', 'x'), 0, 0,...  11 us
    ppermute x1, starting transfers between devices, on_device(): before = lax.ppermute(own, ('zo', 'zi'), [(i, i + 2) for i in range(14)])  5.73 us
    ppermute x1, starting transfers between devices, on_device(): other = lax.ppermute(mine, 'c', [(0, 1), (1, 0)])  4.9 us
    ppermute x1, starting transfers between devices, on_device(): got = lax.ppermute(sent, 'c', [(0, 1), (1, 0)])  2.04 us
    ppermute x1, waiting for transfers between devices, on_device(): lax.ppermute(returned.astype(jnp.bfloat16), ('zo', 'zi'), [(i + 2, i) for...  1.7 us
  transfers between devices with their start and end apart: 4, of which 3 were waited for; matrix products, arithmetic and copies ran while one was open for 0% of the time, Pallas kernels for 10%

profile of v6, /device:TPU:1, one launch (start us, length us, event | category | flops | bytes accessed | tf_op | source)
XLA Modules:
  0.0 84.4 jit_solution(11079585251928874572)
XLA Ops:
  0.6 0.8 fusion
  1.4 5.7 %collective-permute-start = (bf16[144,128]{1,0:T(8,128)(2,1)S(1)}, bf16[144,128]{1,0:T(8,128)(2,1)S(1)}, u32[]{:S(2)}, u32[]{:S(2)}) collective-permute-start(bf16[144,128]{1,0:T(8,128)(2,1)S(1)} %fusion), channel_id=1, source_target_pairs={{0,64},{32,96},{64,128},{96,160},{128,192},{160,224},{192,256},{22... | collective-permute-start | bytes 110600 | tf_op jit(solution)/shard_map/ppermute | solution.py:212
  7.2 1.0 %collective-permute-done = bf16[144,128]{1,0:T(8,128)(2,1)S(1)} collective-permute-done((bf16[144,128]{1,0:T(8,128)(2,1)S(1)}, bf16[144,128]{1,0:T(8,128)(2,1)S(1)}, u32[]{:S(2)}, u32[]{:S(2)}) %collective-permute-start) | collective-permute-done | bytes 36896 | tf_op jit(solution)/shard_map/ppermute | solution.py:212
  8.2 0.1 broadcast_select_fusion
  8.3 0.2 broadcast_in_dim.49
  8.5 0.0 copy-start.3
  8.5 0.0 copy-start
  8.5 0.0 copy-start.1
  8.5 0.0 copy-start.2
  8.5 25.4 %all_to_all.15 = bf16[32,144,128]{2,1,0:T(8,128)(2,1)S(1)} all-to-all(bf16[32,144,128]{2,1,0:T(8,128)(2,1)S(1)} %bitcast.28), channel_id=1, replica_groups=mesh['zo'=8,'zi'=2,'y'=4,'x'=4,'c'=2] {'zi','y','x'}, dimensions={0} | all-to-all | bytes 2359296 | tf_op jit(solution)/shard_map/all_to_all | solution.py:215
  33.9 4.9 %collective-permute-start.1 = (bf16[8,576,128]{2,1,0:T(8,128)(2,1)S(1)}, bf16[8,576,128]{2,1,0:T(8,128)(2,1)}, u32[]{:S(2)}, u32[]{:S(2)}) collective-permute-start(bf16[8,576,128]{2,1,0:T(8,128)(2,1)S(1)} %bitcast.21), channel_id=1, source_target_pairs={{0,1},{1,0},{2,3},{3,2},{4,5},{5,4},{6,7},{7,6},{8,9},{9,8},{10,11... | collective-permute-start | bytes 3538952 | tf_op jit(solution)/shard_map/ppermute | solution.py:218
  38.8 0.0 copy-done.3
  38.8 0.1 pad_add_fusion.meta
  38.9 0.0 copy-done
  38.9 0.0 copy-done.1
  38.9 0.0 copy-done.2
  38.9 2.7 %shard_map.77.e_ref = f32[1032,1024]{1,0:T(8,128)S(1)} custom-call(s32[19]{0:T(128)S(1)} %pad_add_fusion.meta, bf16[8,576,128]{2,1,0:T(8,128)(2,1)S(1)} %bitcast.22, bf16[8,576,128]{2,1,0:T(8,128)(2,1)S(1)} %bitcast.18, bf16[8,576,128]{2,1,0:T(8,128)(2,1)S(1)} %bitcast.24, f32[8,128]{1,0:T(8,128)S(1)} %bitcast.26), custom_call_target="tpu_custom_call" | custom-call | flops 1207959552 | bytes 8388608 | tf_op jit(solution)/shard_map/pallas_call | solution.py:187
  41.6 0.0 collective-permute-done.1.kt_ref.other_ref
  41.6 5.1 %shard_map.78 = (bf16[1024,1024]{1,0:T(8,128)(2,1)S(1)}, bf16[8,288,128]{2,1,0:T(8,128)(2,1)S(1)}) custom-call(s32[19]{0:T(128)S(1)} %pad_add_fusion.meta, bf16[8,576,128]{2,1,0:T(8,128)(2,1)} %collective-permute-done.1.kt_ref.other_ref, bf16[8,576,128]{2,1,0:T(8,128)(2,1)S(1)} %bitcast.19, bf16[8,576,128]{2,1,0:T(8,128)(2,1)S(1)} %bitcast.25, ...), custom_call_target="tpu_custom_call" | custom-call | flops 1811939328 | bytes 8388608 | tf_op jit(solution)/shard_map/pallas_call | solution.py:187
  46.7 2.0 %collective-permute-start.2 = (bf16[8,288,128]{2,1,0:T(8,128)(2,1)S(1)}, bf16[8,288,128]{2,1,0:T(8,128)(2,1)S(1)}, u32[]{:S(2)}, u32[]{:S(2)}) collective-permute-start(bf16[8,288,128]{2,1,0:T(8,128)(2,1)S(1)} %get-tuple-element.7), channel_id=1, source_target_pairs={{0,1},{1,0},{2,3},{3,2},{4,5},{5,4},{6,7},{7,6},{8,9},{9,8},{10,11... | collective-permute-start | bytes 1769480 | tf_op jit(solution)/shard_map/ppermute | solution.py:246
  48.8 1.3 %shard_map.79 = f32[8,288,128]{2,1,0:T(8,128)S(1)} custom-call(s32[19]{0:T(128)S(1)} %pad_add_fusion.meta, bf16[8,576,128]{2,1,0:T(8,128)(2,1)S(1)} %bitcast.20, bf16[1024,1024]{1,0:T(8,128)(2,1)S(1)} %get-tuple-element.6.g_ref), custom_call_target="tpu_custom_call" | custom-call | flops 603979776 | bytes 8388608 | tf_op jit(solution)/shard_map/pallas_call | solution.py:187
  50.1 0.5 collective-permute-done.2
  50.6 0.2 add_convert_fusion
  50.8 14.4 %all_to_all.16 = bf16[32,72,128]{2,1,0:T(8,128)(2,1)S(1)} all-to-all(bf16[32,72,128]{2,1,0:T(8,128)(2,1)S(1)} %bitcast.29), channel_id=1, replica_groups=mesh['zo'=8,'zi'=2,'y'=4,'x'=4,'c'=2] {'zi','y','x'}, dimensions={0} | all-to-all | bytes 1179648 | tf_op jit(solution)/shard_map/all_to_all | solution.py:258
  65.2 0.1 convert_reduce_fusion
  65.3 0.1 select_reduce_fusion
  65.4 1.3 %collective-permute-start.3 = (bf16[72,128]{1,0:T(8,128)(2,1)S(1)}, bf16[72,128]{1,0:T(8,128)(2,1)S(1)}, u32[]{:S(2)}, u32[]{:S(2)}) collective-permute-start(bf16[72,128]{1,0:T(8,128)(2,1)S(1)} %get-tuple-element.10), channel_id=1, source_target_pairs={{64,0},{96,32},{128,64},{160,96},{192,128},{224,160},{256,192},{28... | collective-permute-start | bytes 55304 | tf_op jit(solution)/shard_map/ppermute | solution.py:265
  66.7 4.2 %shard_map.80 = (bf16[8,576,128]{2,1,0:T(8,128)(2,1)}, f32[72,128]{1,0:T(8,128)S(1)}) custom-call(s32[19]{0:T(128)S(1)} %pad_add_fusion.meta, bf16[8,576,128]{2,1,0:T(8,128)(2,1)S(1)} %bitcast.23, bf16[8,576,128]{2,1,0:T(8,128)(2,1)} %collective-permute-done.1.kt_ref.other_ref, bf16[1024,1024]{1,0:T(8,128)(2,1)S(1)} %get-tuple-element.6.g_ref, ...), custom_call_target="tpu_custom_call" | custom-call | flops 1207959552 | bytes 8388608 | tf_op jit(solution)/shard_map/pallas_call | solution.py:187
  71.0 1.7 %collective-permute-done.3 = bf16[72,128]{1,0:T(8,128)(2,1)S(1)} collective-permute-done((bf16[72,128]{1,0:T(8,128)(2,1)S(1)}, bf16[72,128]{1,0:T(8,128)(2,1)S(1)}, u32[]{:S(2)}, u32[]{:S(2)}) %collective-permute-start.3) | collective-permute-done | bytes 18464 | tf_op jit(solution)/shard_map/ppermute | solution.py:265
  72.7 11.0 %all_to_all.17 = bf16[8,72,128]{2,1,0:T(8,128)(2,1)S(1)} all-to-all(bf16[8,72,128]{2,1,0:T(8,128)(2,1)S(1)} %broadcast_in_dim.52), channel_id=1, replica_groups=mesh['zo'=8,'zi'=2,'y'=4,'x'=4,'c'=2] {'c','x'}, dimensions={0} | all-to-all | bytes 294912 | tf_op jit(solution)/shard_map/all_to_all | solution.py:285
  83.7 0.7 copy.9
  (3 shorter events, 0.0 us)
Async XLA Ops:
  1.4 6.8 %collective-permute-start = (bf16[144,128]{1,0:T(8,128)(2,1)S(1)}, bf16[144,128]{1,0:T(8,128)(2,1)S(1)}, u32[]{:S(2)}, u32[]{:S(2)}) collective-permute-start(bf16[144,128]{1,0:T(8,128)(2,1)S(1)} %fusion), channel_id=1, source_target_pairs={{0,64},{32,96},{64,128},{96,160},{128,192},{160,224},{192,256},{22... | collective-permute-start | bytes 110600 | tf_op jit(solution)/shard_map/ppermute | solution.py:212
  8.5 30.3 %copy-start.3 = (s32[16]{0:T(128)S(1)}, s32[16]{0:T(128)}, u32[]{:S(2)}) copy-start(s32[16]{0:T(128)} %param.11) | copy-start | bytes 196
  8.5 30.4 %copy-start = (bf16[128,8,576]{0,2,1:T(8,128)(2,1)S(1)}, bf16[128,8,576]{0,2,1:T(8,128)(2,1)}, u32[]{:S(2)}) copy-start(bf16[128,8,576]{0,2,1:T(8,128)(2,1)} %param.6) | copy-start | bytes 3538948
  8.5 30.4 %copy-start.1 = (bf16[128,8,576]{0,2,1:T(8,128)(2,1)S(1)}, bf16[128,8,576]{0,2,1:T(8,128)(2,1)}, u32[]{:S(2)}) copy-start(bf16[128,8,576]{0,2,1:T(8,128)(2,1)} %param.7) | copy-start | bytes 3538948
  8.5 30.4 %copy-start.2 = (f32[128,8]{0,1:T(8,128)S(1)}, f32[128,8]{0,1:T(8,128)}, u32[]{:S(2)}) copy-start(f32[128,8]{0,1:T(8,128)} %param.10) | copy-start | bytes 12292
  33.9 7.7 %collective-permute-start.1 = (bf16[8,576,128]{2,1,0:T(8,128)(2,1)S(1)}, bf16[8,576,128]{2,1,0:T(8,128)(2,1)}, u32[]{:S(2)}, u32[]{:S(2)}) collective-permute-start(bf16[8,576,128]{2,1,0:T(8,128)(2,1)S(1)} %bitcast.21), channel_id=1, source_target_pairs={{0,1},{1,0},{2,3},{3,2},{4,5},{5,4},{6,7},{7,6},{8,9},{9,8},{10,11... | collective-permute-start | bytes 3538952 | tf_op jit(solution)/shard_map/ppermute | solution.py:218
  46.7 3.9 %collective-permute-start.2 = (bf16[8,288,128]{2,1,0:T(8,128)(2,1)S(1)}, bf16[8,288,128]{2,1,0:T(8,128)(2,1)S(1)}, u32[]{:S(2)}, u32[]{:S(2)}) collective-permute-start(bf16[8,288,128]{2,1,0:T(8,128)(2,1)S(1)} %get-tuple-element.7), channel_id=1, source_target_pairs={{0,1},{1,0},{2,3},{3,2},{4,5},{5,4},{6,7},{7,6},{8,9},{9,8},{10,11... | collective-permute-start | bytes 1769480 | tf_op jit(solution)/shard_map/ppermute | solution.py:246
  65.4 7.2 %collective-permute-start.3 = (bf16[72,128]{1,0:T(8,128)(2,1)S(1)}, bf16[72,128]{1,0:T(8,128)(2,1)S(1)}, u32[]{:S(2)}, u32[]{:S(2)}) collective-permute-start(bf16[72,128]{1,0:T(8,128)(2,1)S(1)} %get-tuple-element.10), channel_id=1, source_target_pairs={{64,0},{96,32},{128,64},{160,96},{192,128},{224,160},{256,192},{28... | collective-permute-start | bytes 55304 | tf_op jit(solution)/shard_map/ppermute | solution.py:265
